TPU v7x, 256 devices: a whole 4x4x8 slice. The times are simulated.
256 devices in a mesh: adapter: 32 (over x, y, core), tensor: 8 (over z).
Axes of the slice: x: 4, y: 4, z: 8, core: 2. Of those that a mesh axis runs over, the one named last changes fastest.
Arguments:
- activations: bfloat16 [49152, 8192], P('adapter', 'tensor'), may hold values from -6 to 6
- output_gradient: bfloat16 [49152, 1024], P('adapter', 'tensor'), may hold values from -1.5 to 1.5
- adapter_of_row: int32 [49152, 1], P('adapter'), may hold values from 0 to 127; in each aligned block of 1536 rows (0 to 1535, 1536 to 3071, ...) at most 15 rows name the same one
- frozen_value_weight: bfloat16 [8192, 1024], P('tensor'), may hold values from -0.1875 to 0.1875
- adapter_down_weight: bfloat16 [128, 64, 8192], P('adapter', None, 'tensor'), may hold values from -0.0625 to 0.0625
- adapter_up_weight: bfloat16 [128, 64, 1024], P('adapter', None, 'tensor'), may hold values from -0.1875 to 0.1875
Outputs:
- input_gradient: bfloat16 [49152, 8192], P('adapter', 'tensor')
- down_gradient: float32 [128, 64, 8192], P('adapter', None, 'tensor')
- up_gradient: float32 [128, 64, 1024], P('adapter', None, 'tensor')
Inputs may be any that keep to these rules, and one draw needn't show every extreme that they name: `adapter_of_row`: among the rows of one device no adapter id appears more than 15 times, and in every draw some adapter appears exactly 15 times among some device's rows. Every adapter appears somewhere.
All inputs are finite; a program needn't handle non-finite values.
Results may differ from a plain program's by a relative error of at most 0.0034.
Values may be sent and summed in bfloat16 or wider, within the bound.
A program may use at most 128 MiB of HBM per device.

v0:
```python
import jax
import jax.numpy as jnp
from jax import lax
from jax.sharding import PartitionSpec as P

adapter_scale = 2.0


def base_gradient(output_gradient, frozen_value_weight):
    return lax.dot_general(
        lax.all_gather(output_gradient, "tensor", axis=1, tiled=True),
        frozen_value_weight,
        (((1,), (1,)), ((), ())),
        preferred_element_type=jnp.float32,
    )


def body(
    activations,
    output_gradient,
    adapter_of_row,
    frozen_value_weight,
    adapter_down_weight,
    adapter_up_weight,
):
    tok_rows = activations.shape[0]
    input_width = activations.shape[1]
    width_k = output_gradient.shape[1]
    owner_devices = lax.axis_size("adapter")
    rows_each_owner = adapter_down_weight.shape[0]
    adapters_all = owner_devices * rows_each_owner
    row_capacity = 5 * tok_rows // (4 * adapters_all)
    rank_dimension = adapter_down_weight.shape[1]
    token_ids = adapter_of_row[:, 0]
    onehot = (token_ids[:, None] == jnp.arange(adapters_all, dtype=jnp.int32)[None, :]).astype(
        jnp.int32
    )
    position = jnp.sum(jnp.cumsum(onehot, axis=0) * onehot, axis=1) - 1
    owner_slot_index = token_ids * row_capacity + position
    send_rows = (
        jnp.zeros((adapters_all * row_capacity, input_width), jnp.bfloat16)
        .at[owner_slot_index]
        .set(activations)
    )
    send_rows = send_rows.reshape(owner_devices, rows_each_owner * row_capacity, input_width)
    send_grads = (
        jnp.zeros((adapters_all * row_capacity, width_k), jnp.bfloat16)
        .at[owner_slot_index]
        .set(output_gradient)
    )
    send_grads = send_grads.reshape(owner_devices, rows_each_owner * row_capacity, width_k)
    dispatched_rows = lax.all_to_all(send_rows, "adapter", split_axis=0, concat_axis=0, tiled=True)
    dispatched_gradients = lax.all_to_all(
        send_grads, "adapter", split_axis=0, concat_axis=0, tiled=True
    )
    dispatched_rows = dispatched_rows.reshape(
        owner_devices, rows_each_owner, row_capacity, input_width
    )
    dispatched_gradients = dispatched_gradients.reshape(
        owner_devices, rows_each_owner, row_capacity, width_k
    )
    low_part = jnp.einsum(
        "zbnu,bgu->zbng", dispatched_rows, adapter_down_weight, preferred_element_type=jnp.float32
    )
    back_part = jnp.einsum(
        "coeq,oyq->coey",
        dispatched_gradients,
        adapter_up_weight,
        preferred_element_type=jnp.float32,
    )
    rank_total = lax.psum(jnp.concatenate([low_part, back_part], axis=3), "tensor")
    rank_value = rank_total[..., :rank_dimension].astype(jnp.bfloat16)
    value_backward = rank_total[..., rank_dimension:].astype(jnp.bfloat16)
    down_gradient = adapter_scale * jnp.einsum(
        "sapr,sapf->arf", value_backward, dispatched_rows, preferred_element_type=jnp.float32
    )
    up_gradient = adapter_scale * jnp.einsum(
        "sapr,sapk->ark", rank_value, dispatched_gradients, preferred_element_type=jnp.float32
    )
    adapter_share = (
        adapter_scale
        * jnp.einsum(
            "hwec,wcu->hweu",
            value_backward,
            adapter_down_weight,
            preferred_element_type=jnp.float32,
        )
    ).astype(jnp.bfloat16)
    returned_gradient = lax.all_to_all(
        adapter_share.reshape(owner_devices, rows_each_owner * row_capacity, input_width),
        "adapter",
        split_axis=0,
        concat_axis=0,
        tiled=True,
    )
    returned_gradient = returned_gradient.reshape(adapters_all * row_capacity, input_width)
    adapter_rows = returned_gradient[owner_slot_index]
    frozen_share = base_gradient(output_gradient, frozen_value_weight)
    input_gradient = (frozen_share + adapter_rows.astype(jnp.float32)).astype(jnp.bfloat16)
    return (input_gradient, down_gradient, up_gradient)


def solution(mesh):
    in_specs = (
        P("adapter", "tensor"),
        P("adapter", "tensor"),
        P("adapter", None),
        P("tensor", None),
        P("adapter", None, "tensor"),
        P("adapter", None, "tensor"),
    )
    out_specs = (P("adapter", "tensor"), P("adapter", None, "tensor"), P("adapter", None, "tensor"))
    return jax.shard_map(body, mesh=mesh, in_specs=in_specs, out_specs=out_specs, check_vma=False)
```

profile of v0, /device:TPU:6, one launch (start us, length us, event | category | flops | bytes accessed | tf_op | source)
XLA Modules:
  0.0 245.0 jit_solution(8599779141236210584)
XLA Ops:
  7.2 0.9 reduce
  9.4 4.9 %scatter_custom_fusion.1 = bf16[1920,128]{1,0:T(8,128)(2,1)S(1)} fusion(s32[1536]{0:T(1024)S(1)} %fusion.16, bf16[1536,128]{1,0:T(8,128)(2,1)} %param.7, bf16[]{:T(256)} %constant.6.clone.1), kind=kCustom, calls=%fused_computation.27 | custom fusion | bytes 492032 | tf_op jit(solution)/shard_map/scatter | solution.py:49
  14.4 0.9 reshape.52
  15.3 7.6 %all-to-all-start.1 = ((bf16[32,60,128]{2,1,0:T(8,128)(2,1)}), bf16[32,60,128]{2,1,0:T(8,128)(2,1)S(1)}, u32[]{:S(2)}, u32[]{:S(2)}) async-start(bf16[32,60,128]{2,1,0:T(8,128)(2,1)} %reshape.52), calls=%async_computation.1 | async-start | bytes 1048576 | tf_op jit(solution)/shard_map/all_to_all | solution.py:53
  22.9 10.7 %scatter_custom_fusion = bf16[1920,1024]{1,0:T(8,128)(2,1)} fusion(s32[1536]{0:T(1024)S(1)} %fusion.16, bf16[1536,1024]{1,0:T(8,128)(2,1)} %param.6, bf16[]{:T(256)} %constant.6.clone.1), kind=kCustom, calls=%fused_computation.5 | custom fusion | bytes 3932672 | tf_op jit(solution)/shard_map/scatter | solution.py:43
  33.6 5.9 %reshape.50 = bf16[32,60,1024]{2,1,0:T(8,128)(2,1)} reshape(bf16[1920,1024]{1,0:T(8,128)(2,1)} %scatter_custom_fusion) | data formatting | bytes 7864320 | tf_op jit(solution)/shard_map/reshape | solution.py:45
  39.5 7.6 %all-to-all-start = ((bf16[32,60,1024]{2,1,0:T(8,128)(2,1)}), bf16[32,60,1024]{2,1,0:T(8,128)(2,1)}, u32[]{:S(2)}, u32[]{:S(2)}) async-start(bf16[32,60,1024]{2,1,0:T(8,128)(2,1)} %reshape.50), calls=%async_computation | async-start | bytes 8388608 | tf_op jit(solution)/shard_map/all_to_all | solution.py:52
  47.3 0.5 all-gather.2.cloned.1.call-update
  48.2 0.8 copy-done.2
  49.2 49.0 %all-to-all-done = bf16[32,60,1024]{2,1,0:T(8,128)(2,1)} async-done(((bf16[32,60,1024]{2,1,0:T(8,128)(2,1)}), bf16[32,60,1024]{2,1,0:T(8,128)(2,1)}, u32[]{:S(2)}, u32[]{:S(2)}) %all-to-all-start) | async-done | bytes 3932192 | tf_op jit(solution)/shard_map/all_to_all | solution.py:52
  98.2 4.4 %copy.13 = bf16[32,60,1024]{2,0,1:T(8,128)(2,1)S(1)} copy(bf16[32,60,1024]{2,1,0:T(8,128)(2,1)} %all-to-all-done) | data formatting | bytes 7864320 | tf_op jit(solution)/shard_map/all_to_all | solution.py:52
  102.7 1.2 convolution_bitcast_fusion.2
  103.8 0.7 copy-done.1
  104.5 1.3 pad_maximum_fusion
  105.8 42.9 %all-reduce.1 = bf16[32,4,15,128]{3,0,2,1:T(8,128)(2,1)S(1)} all-reduce(f32[32,4,15,128]{3,0,2,1:T(8,128)} %pad_maximum_fusion), channel_id=1, replica_groups=mesh['adapter'=32,'tensor'=8] {'tensor'}, use_global_device_ids=true, to_apply=%region_5.6 | all-reduce | flops 245760 | bytes 1474560 | tf_op jit(solution)/shard_map/psum | solution.py:71
  148.8 2.3 multiply_convert_fusion
  151.0 4.2 %copy.15 = bf16[32,60,1024]{2,1,0:T(8,128)(2,1)} copy(bf16[32,60,1024]{2,0,1:T(8,128)(2,1)S(1)} %bitcast.49) | data formatting | bytes 7864320 | tf_op jit(solution)/shard_map/reshape | solution.py:90
  155.2 8.3 %all-to-all-start.2 = ((bf16[32,60,1024]{2,1,0:T(8,128)(2,1)}), bf16[32,60,1024]{2,1,0:T(8,128)(2,1)}, u32[]{:S(2)}, u32[]{:S(2)}) async-start(bf16[32,60,1024]{2,1,0:T(8,128)(2,1)} %copy.15), calls=%async_computation.2 | async-start | bytes 8388608 | tf_op jit(solution)/shard_map/all_to_all | solution.py:89
  163.6 1.0 fusion.3
  164.6 4.2 %fusion.2 = f32[4,64,1024]{2,1,0:T(8,128)} fusion(bf16[32,4,15,1024]{3,0,2,1:T(8,128)(2,1)} %bitcast.48, bf16[32,4,15,128]{3,0,2,1:T(8,128)(2,1)S(1)} %all-reduce.1), kind=kOutput, calls=%fused_computation.8 | convolution fusion | flops 251920384 | bytes 5472256 | tf_op jit(solution)/shard_map/sapr,sapf->arf/dot_general | solution.py:74
  168.8 45.8 %all-to-all-done.2 = bf16[32,60,1024]{2,1,0:T(8,128)(2,1)} async-done(((bf16[32,60,1024]{2,1,0:T(8,128)(2,1)}), bf16[32,60,1024]{2,1,0:T(8,128)(2,1)}, u32[]{:S(2)}, u32[]{:S(2)}) %all-to-all-start.2) | async-done | bytes 3932192 | tf_op jit(solution)/shard_map/all_to_all | solution.py:89
  214.6 5.9 %reshape.55 = bf16[1920,1024]{1,0:T(8,128)(2,1)} reshape(bf16[32,60,1024]{2,1,0:T(8,128)(2,1)} %all-to-all-done.2) | data formatting | bytes 7864320 | tf_op jit(solution)/shard_map/reshape | solution.py:96
  220.6 10.4 %gather_fusion = bf16[1536,1024]{1,0:T(8,128)(2,1)} fusion(bf16[1920,1024]{1,0:T(8,128)(2,1)} %reshape.55, s32[2048]{0:T(1024)S(1)} %pad_clamp_fusion), kind=kCustom, calls=%fused_computation | custom fusion | bytes 6297600 | tf_op jit(solution)/shard_map/gather | solution.py:97
  230.9 7.2 %add_convert_fusion = bf16[1536,1024]{1,0:T(8,128)(2,1)} fusion(bf16[1536,1024]{1,0:T(8,128)(2,1)} %gather_fusion, bf16[1536,1024]{1,0:T(8,128)(2,1)} %all-gather.2.cloned.1.call-done, bf16[1024,1024]{1,0:T(8,128)(2,1)S(1)} %copy-done), kind=kOutput, calls=%fused_computation.4 | convolution fusion | flops 3225944064 | bytes 11534336 | tf_op jit(solution)/shard_map/dot_general | solution.py:10
  (27 shorter events, 2.2 us)
Async XLA Ops:
  7.2 223.8 %copy-start = (bf16[1024,1024]{1,0:T(8,128)(2,1)S(1)}, bf16[1024,1024]{1,0:T(8,128)(2,1)}, u32[]{:S(2)}) copy-start(bf16[1024,1024]{1,0:T(8,128)(2,1)} %param.9) | copy-start | bytes 6291460
  7.2 2.2 copy-start.6
  15.3 24.2 %all-to-all-start.1 = ((bf16[32,60,128]{2,1,0:T(8,128)(2,1)}), bf16[32,60,128]{2,1,0:T(8,128)(2,1)S(1)}, u32[]{:S(2)}, u32[]{:S(2)}) async-start(bf16[32,60,128]{2,1,0:T(8,128)(2,1)} %reshape.52), calls=%async_computation.1 | async-start | bytes 1048576 | tf_op jit(solution)/shard_map/all_to_all | solution.py:53
  39.5 9.4 %copy-start.5 = (bf16[4,64,128]{2,1,0:T(8,128)(2,1)S(1)}, bf16[4,64,128]{2,1,0:T(8,128)(2,1)}, u32[]{:S(2)}) copy-start(bf16[4,64,128]{2,1,0:T(8,128)(2,1)} %param.11) | copy-start | bytes 196612
  39.5 58.7 %all-to-all-start = ((bf16[32,60,1024]{2,1,0:T(8,128)(2,1)}), bf16[32,60,1024]{2,1,0:T(8,128)(2,1)}, u32[]{:S(2)}, u32[]{:S(2)}) async-start(bf16[32,60,1024]{2,1,0:T(8,128)(2,1)} %reshape.50), calls=%async_computation | async-start | bytes 8388608 | tf_op jit(solution)/shard_map/all_to_all | solution.py:52
  47.1 183.9 %all-gather.2.cloned.1.call-start = ((), (), s32[]{:S(2)}) async-start(), calls=%async_computation.3 | async-start | bytes 3538944 | tf_op jit(solution)/shard_map/all_gather | solution.py:11
  48.1 0.8 copy-start.2
  98.2 4.4 %copy-start.4 = (bf16[4,64,1024]{2,1,0:T(8,128)(2,1)S(1)}, bf16[4,64,1024]{2,1,0:T(8,128)(2,1)}, u32[]{:S(2)}) copy-start(bf16[4,64,1024]{2,1,0:T(8,128)(2,1)} %param.10) | copy-start | bytes 1572868
  102.6 1.9 copy-start.1
  155.2 8.4 %copy-start.3 = (bf16[32,60,128]{2,0,1:T(8,128)(2,1)S(1)}, bf16[32,60,128]{2,0,1:T(8,128)(2,1)}, u32[]{:S(2)}) copy-start(bf16[32,60,128]{2,0,1:T(8,128)(2,1)} %copy-done.2) | copy-start | bytes 1474564
  155.2 59.4 %all-to-all-start.2 = ((bf16[32,60,1024]{2,1,0:T(8,128)(2,1)}), bf16[32,60,1024]{2,1,0:T(8,128)(2,1)}, u32[]{:S(2)}, u32[]{:S(2)}) async-start(bf16[32,60,1024]{2,1,0:T(8,128)(2,1)} %copy.15), calls=%async_computation.2 | async-start | bytes 8388608 | tf_op jit(solution)/shard_map/all_to_all | solution.py:89
Sparse Core Ops, SparseCore 0:
  49.6 56.5 all-gather.1
where the time goes:
time: 249 us; the launch traced here: 245 us
  waiting for transfers between devices  95.3 us (38%)
  local copies, waits for them, and re-layouts  49.5 us (20%)
  blocking collectives  42.9 us (17%)
  starting transfers between devices  23.7 us (10%)
  matrix products  16.1 us (6%)
  between operations  14.2 us (6%)
  other arithmetic  3.11 us (1%)
    all_to_all x1, waiting for transfers between devices, body(): lax.all_to_all(send_rows, 'adapter', split_axis=0, concat_axis=0, tiled=T...  49 us
    all_to_all x1, waiting for transfers between devices, body(): lax.all_to_all(adapter_share.reshape(owner_devices, rows_each_owner * row...  45.8 us
    psum x1, blocking collectives, body(): lax.psum(jnp.concatenate([low_part, back_part], axis=3), 'tensor')  42.9 us
    scatter x1, local copies, waits for them, and re-layouts, body(): send_rows = jnp.zeros((adapters_all * row_capacity, input_width), jnp.bfl...  10.7 us
    gather x1, local copies, waits for them, and re-layouts, body(): adapter_rows = returned_gradient[owner_slot_index]  10.4 us
    all_to_all x1, starting transfers between devices, body(): lax.all_to_all(adapter_share.reshape(owner_devices, rows_each_owner * row...  8.33 us
    all_to_all x1, starting transfers between devices, body(): lax.all_to_all(send_grads, 'adapter', split_axis=0, concat_axis=0, tiled=...  7.61 us
    all_to_all x1, starting transfers between devices, body(): lax.all_to_all(send_rows, 'adapter', split_axis=0, concat_axis=0, tiled=T...  7.57 us
  transfers between devices with their start and end apart: 4, of which 2 were waited for; matrix products, arithmetic and copies ran while one was open for 21% of the time, Pallas kernels for 0%

commit v1 on v0

v1 whole, which is shorter than its diff:
```python
import jax
import jax.numpy as jnp
from jax import lax
from jax.experimental import pallas as pl
from jax.experimental.pallas import tpu as pltpu
from jax.sharding import PartitionSpec as P

adapter_scale = 2.0
MESH = pl.DeviceIdType.MESH
BF = jnp.bfloat16
F32 = jnp.float32

MOST = 15
SLOTS = 240
HALF = 512
ROWS = 1536
RANK = 64
GW = 128
OWN = 256

(U_A, U_B, G_A, G_B, D_A, D_B, X_A, X_B, B_RS, B_AG, L_RS, L_AG, R_A, R_B, DG_A, DG_B, UG_A, UG_B) = range(18)


def rank_kernel(
    x_ref, g_ref, sa_ref, sb_ref, d_ref, u_ref,
    reta_ref, retb_ref, down_ref, up_ref,
    sxa, sxb, sga, sgb, rxa, rxb, rga, rgb,
    da, db, ua, ub,
    maskf, maskb,
    bpart, bz, bsum, ball, lpart, lz, lsum, lall,
    ma, mb, outa, outb,
    dga, dgb, dgra, dgrb, dgo, uga, ugb, ugra, ugrb, ugo,
    ss, rs, loc,
):
    a = lax.axis_index("adapter")
    z = lax.axis_index("tensor")
    c = a % 2
    y = (a // 2) % 4
    x = a // 8
    m_a = y * 2 + c
    m_b = x * 2 + c

    def on_a(t):
        return ((x * 4 + t // 2) * 2 + t % 2, z)

    def on_b(t):
        return (((t // 2) * 4 + y) * 2 + t % 2, z)

    def ring_x(t):
        return ((t * 4 + y) * 2 + c, z)

    def ring_y(t):
        return ((x * 4 + t) * 2 + c, z)

    def ring_z(t):
        return (a, t)

    def copy(kind, src, dst, to, me, device):
        return pltpu.make_async_remote_copy(
            src_ref=src, dst_ref=dst, send_sem=ss.at[kind, to], recv_sem=rs.at[kind, me],
            device_id=device, device_id_type=MESH,
        )

    def arrived(kind, dst, frm):
        pltpu.make_async_remote_copy(
            src_ref=dst, dst_ref=dst, send_sem=ss.at[kind, frm], recv_sem=rs.at[kind, frm],
            device_id=(a, z), device_id_type=MESH,
        ).wait_recv()

    def left(kind, src, to):
        pltpu.make_async_remote_copy(
            src_ref=src, dst_ref=src, send_sem=ss.at[kind, to], recv_sem=rs.at[kind, to],
            device_id=(a, z), device_id_type=MESH,
        ).wait_send()

    barrier = pltpu.get_barrier_semaphore()

    @pl.loop(1, 8)
    def _(d):
        pl.semaphore_signal(barrier, inc=1, device_id=on_a((m_a + d) % 8), device_id_type=MESH)
        pl.semaphore_signal(barrier, inc=1, device_id=ring_z((z + d) % 8), device_id_type=MESH)

    @pl.loop(2, 8)
    def _(d):
        t = ((x * 2) + d) % 8
        pl.semaphore_signal(barrier, inc=1, device_id=on_b(t), device_id_type=MESH)

    pl.semaphore_wait(barrier, 20)

    @pl.loop(1, 4)
    def _(d):
        tx = (x + d) % 4
        ty = (y + d) % 4
        copy(U_A, u_ref, ua.at[x], tx, x, ring_x(tx)).start()
        copy(U_B, u_ref, ub.at[y], ty, y, ring_y(ty)).start()

    ua[x] = u_ref[...]
    ub[y] = u_ref[...]

    slot_rows = lax.broadcasted_iota(jnp.int32, (SLOTS, ROWS), 0)

    def choose(s_ref, t):
        return jnp.where(slot_rows + t * SLOTS == s_ref[...], 1.0, 0.0).astype(BF)

    def route(kind, m, on, s_ref, value, send, recv, d):
        t = (m + d) % 8
        block = jnp.dot(choose(s_ref, t), value, preferred_element_type=F32).astype(BF)

        @pl.when(d == 0)
        def _():
            recv[m] = block

        @pl.when(d != 0)
        def _():
            send[t] = block
            copy(kind, send.at[t], recv.at[m], t, m, on(t)).start()

    def near_first(k):
        return jnp.where(k < 4, 2 + 4 * (k % 2) + k // 2, 4 * (1 - (k - 4) // 2) + k % 2)

    @pl.loop(0, 8)
    def _(k):
        d = near_first(k)
        route(G_A, m_a, on_a, sa_ref, g_ref[...], sga, rga, d)
        route(G_B, m_b, on_b, sb_ref, g_ref[...], sgb, rgb, d)

    @pl.loop(1, 4)
    def _(d):
        tx = (x + d) % 4
        ty = (y + d) % 4
        copy(D_A, d_ref.at[:, pl.ds(0, HALF)], da.at[x], tx, x, ring_x(tx)).start()
        copy(D_B, d_ref.at[:, pl.ds(HALF, HALF)], db.at[y], ty, y, ring_y(ty)).start()

    da[x] = d_ref[:, :HALF]
    db[y] = d_ref[:, HALF:]

    @pl.loop(0, 8)
    def _(k):
        d = near_first(k)
        route(X_A, m_a, on_a, sa_ref, x_ref[:, :HALF], sxa, rxa, d)
        route(X_B, m_b, on_b, sb_ref, x_ref[:, HALF:], sxb, rxb, d)

    first = (lax.broadcasted_iota(jnp.int32, (SLOTS, 1024), 1) >> 6) * MOST
    row = lax.broadcasted_iota(jnp.int32, (SLOTS, 1024), 0)
    mask = jnp.where((row >= first) & (row < first + MOST), 1.0, 0.0)
    maskf[...] = mask
    maskb[...] = mask.astype(BF)
    low_lanes = lax.broadcasted_iota(jnp.int32, (SLOTS, 128), 1) < RANK

    def fold(rows, weights):
        product = lax.dot_general(rows, weights, (((1,), (1,)), ((), ())), preferred_element_type=F32)
        product = product * maskf[...]
        total = product[:, :128]
        for i in range(1, 8):
            total = total + product[:, i * 128 : (i + 1) * 128]
        return total + pltpu.roll(total, RANK, 1)

    def pair(rows_a, weights_a, rows_b, weights_b):
        return jnp.where(low_lanes, fold(rows_a, weights_a), fold(rows_b, weights_b))

    def spread(both, is_a):
        wide = both.astype(F32)
        turned = pltpu.roll(wide, RANK, 1)
        one = (jnp.where(low_lanes, wide, turned) if is_a else jnp.where(low_lanes, turned, wide)).astype(BF)
        return jnp.concatenate([one] * 8, axis=1) * maskb[...]

    @pl.loop(1, 4)
    def _(d):
        fx = (x + d) % 4
        fy = (y + d) % 4
        arrived(U_A, ua.at[fx], fx)
        arrived(U_B, ub.at[fy], fy)

    @pl.loop(1, 8)
    def _(d):
        fa = (m_a + d) % 8
        fb = (m_b + d) % 8
        arrived(G_A, rga.at[fa], fa)
        arrived(G_B, rgb.at[fb], fb)

    def partial_sums(kind, part, held, k, rows_a, weights_a, rows_b, weights_b):
        t = (z + k) % 8
        value = pair(rows_a[t], weights_a[...].reshape(1024, -1), rows_b[t], weights_b[...].reshape(1024, -1))

        @pl.when(k == 0)
        def _():
            held[z] = value

        @pl.when(k != 0)
        def _():
            part[t] = value
            copy(kind, part.at[t], held.at[z], t, z, ring_z(t)).start()

    @pl.loop(0, 8)
    def _(k):
        partial_sums(B_RS, bpart, bz, k, rga, ua, rgb, ub)

    @pl.loop(1, 4)
    def _(d):
        fx = (x + d) % 4
        fy = (y + d) % 4
        arrived(D_A, da.at[fx], fx)
        arrived(D_B, db.at[fy], fy)

    @pl.loop(1, 8)
    def _(d):
        fa = (m_a + d) % 8
        fb = (m_b + d) % 8
        arrived(X_A, rxa.at[fa], fa)
        arrived(X_B, rxb.at[fb], fb)

    def finish_sums(rs_kind, ag_kind, held, total, everything):
        @pl.loop(1, 8)
        def _(d):
            t = (z + d) % 8
            arrived(rs_kind, held.at[t], t)

        acc = held[0]
        for i in range(1, 8):
            acc = acc + held[i]
        total[...] = acc.astype(BF)
        everything[z] = acc.astype(BF)

        @pl.loop(1, 8)
        def _(d):
            t = (z + d) % 8
            copy(ag_kind, total, everything.at[z], t, z, ring_z(t)).start()

    finish_sums(B_RS, B_AG, bz, bsum, ball)

    @pl.loop(0, 8)
    def _(k):
        partial_sums(L_RS, lpart, lz, k, rxa, da, rxb, db)

    @pl.loop(1, 8)
    def _(d):
        t = (z + d) % 8
        arrived(B_AG, ball.at[t], t)

    def give_back(kind, m, on, masked, is_a, weights, out, ret, d):
        s = (m + d) % 8
        block = spread(ball[s], is_a)
        masked[s] = block
        out[s] = (
            adapter_scale * jnp.dot(block, weights[...].reshape(1024, HALF), preferred_element_type=F32)
        ).astype(BF)

        @pl.when(d != 0)
        def _():
            copy(kind, out.at[s], ret.at[m], s, m, on(s)).start()

        @pl.when(d == 0)
        def _():
            pltpu.make_async_copy(out.at[s], ret.at[m], loc.at[kind - R_A]).start()

    @pl.loop(0, 8)
    def _(k):
        d = near_first(k)
        give_back(R_A, m_a, on_a, ma, True, da, outa, reta_ref, d)
        give_back(R_B, m_b, on_b, mb, False, db, outb, retb_ref, d)

    def gradient(masked, rows, q):
        return adapter_scale * lax.dot_general(
            masked[:, :, pl.ds(pl.multiple_of(q * OWN, OWN), OWN)].reshape(8 * SLOTS, OWN),
            rows[...].reshape(8 * SLOTS, -1),
            (((0,), (0,)), ((), ())),
            preferred_element_type=F32,
        )

    def to_owner(kind, m, ring, masked, rows, part, recv, own, half, d):
        q = (m + d) % 4
        value = gradient(masked, rows, q)

        @pl.when(d == 4)
        def _():
            own[half] = value

        @pl.when(d != 4)
        def _():
            part[q] = value.astype(part.dtype)
            copy(kind, part.at[q], recv.at[m], q, m, ring(q)).start()

    @pl.loop(1, 5)
    def _(d):
        to_owner(DG_A, x, ring_x, ma, rxa, dga, dgra, dgo, 0, d)
        to_owner(DG_B, y, ring_y, mb, rxb, dgb, dgrb, dgo, 1, d)

    finish_sums(L_RS, L_AG, lz, lsum, lall)

    @pl.loop(1, 8)
    def _(d):
        t = (z + d) % 8
        arrived(L_AG, lall.at[t], t)

    @pl.loop(0, 8)
    def _(s):
        ma[s] = spread(lall[s], True)
        mb[s] = spread(lall[s], False)

    @pl.loop(1, 5)
    def _(d):
        to_owner(UG_A, x, ring_x, ma, rga, uga, ugra, ugo, 0, d)
        to_owner(UG_B, y, ring_y, mb, rgb, ugb, ugrb, ugo, 1, d)

    @pl.loop(1, 4)
    def _(d):
        fx = (x + d) % 4
        fy = (y + d) % 4
        arrived(DG_A, dgra.at[fx], fx)
        arrived(DG_B, dgrb.at[fy], fy)
        dgo[0] += dgra[fx].astype(F32)
        dgo[1] += dgrb[fy].astype(F32)

    down_ref[:, :HALF] = dgo[0]
    down_ref[:, HALF:] = dgo[1]

    @pl.loop(1, 4)
    def _(d):
        fx = (x + d) % 4
        fy = (y + d) % 4
        arrived(UG_A, ugra.at[fx], fx)
        arrived(UG_B, ugrb.at[fy], fy)
        ugo[0] += ugra[fx]
        ugo[1] += ugrb[fy]

    up_ref[...] = ugo[0] + ugo[1]

    @pl.loop(1, 8)
    def _(d):
        ta = (m_a + d) % 8
        tb = (m_b + d) % 8
        tz = (z + d) % 8
        arrived(R_A, reta_ref.at[ta], ta)
        arrived(R_B, retb_ref.at[tb], tb)
        left(G_A, sga.at[ta], ta)
        left(G_B, sgb.at[tb], tb)
        left(X_A, sxa.at[ta], ta)
        left(X_B, sxb.at[tb], tb)
        left(R_A, outa.at[ta], ta)
        left(R_B, outb.at[tb], tb)
        left(B_RS, bpart.at[tz], tz)
        left(L_RS, lpart.at[tz], tz)
        left(B_AG, bsum, tz)
        left(L_AG, lsum, tz)

    @pl.loop(1, 4)
    def _(d):
        tx = (x + d) % 4
        ty = (y + d) % 4
        left(U_A, u_ref, tx)
        left(U_B, u_ref, ty)
        left(D_A, d_ref.at[:, pl.ds(0, HALF)], tx)
        left(D_B, d_ref.at[:, pl.ds(HALF, HALF)], ty)
        left(DG_A, dga.at[tx], tx)
        left(DG_B, dgb.at[ty], ty)
        left(UG_A, uga.at[tx], tx)
        left(UG_B, ugb.at[ty], ty)

    pltpu.make_async_copy(outa.at[m_a], reta_ref.at[m_a], loc.at[0]).wait()
    pltpu.make_async_copy(outb.at[m_b], retb_ref.at[m_b], loc.at[1]).wait()


def rank_part(x, g, slot_a, slot_b, d, u):
    vmem = pl.BlockSpec(memory_space=pltpu.VMEM)
    hbm = pl.BlockSpec(memory_space=pl.ANY)
    block = lambda width, dtype=BF: pltpu.VMEM((8, SLOTS, width), dtype)
    chunk = lambda width, dtype=BF: pltpu.VMEM((4, OWN, width), dtype)
    return pl.pallas_call(
        rank_kernel,
        out_shape=(
            jax.ShapeDtypeStruct((8, SLOTS, HALF), BF),
            jax.ShapeDtypeStruct((8, SLOTS, HALF), BF),
            jax.ShapeDtypeStruct((OWN, 2 * HALF), F32),
            jax.ShapeDtypeStruct((OWN, GW), F32),
        ),
        in_specs=[vmem] * 6,
        out_specs=(hbm, hbm, vmem, vmem),
        scratch_shapes=[
            block(HALF), block(HALF), block(GW), block(GW),
            block(HALF), block(HALF), block(GW), block(GW),
            chunk(HALF), chunk(HALF), chunk(GW), chunk(GW),
            pltpu.VMEM((SLOTS, 1024), F32), pltpu.VMEM((SLOTS, 1024), BF),
            block(128, F32), block(128, F32), pltpu.VMEM((SLOTS, 128), BF), block(128),
            block(128, F32), block(128, F32), pltpu.VMEM((SLOTS, 128), BF), block(128),
            block(1024), block(1024), block(HALF), block(HALF),
            chunk(HALF), chunk(HALF), chunk(HALF), chunk(HALF), pltpu.VMEM((2, OWN, HALF), F32),
            chunk(GW, F32), chunk(GW, F32), chunk(GW, F32), chunk(GW, F32), pltpu.VMEM((2, OWN, GW), F32),
            pltpu.SemaphoreType.DMA((18, 8)), pltpu.SemaphoreType.DMA((18, 8)), pltpu.SemaphoreType.DMA((2,)),
        ],
        compiler_params=pltpu.CompilerParams(
            collective_id=0, has_side_effects=True, vmem_limit_bytes=60 * 2**20
        ),
        cost_estimate=pl.CostEstimate(flops=30 * 10**9, bytes_accessed=20 * 10**6, transcendentals=0),
        name="rank_part",
    )(x, g, slot_a, slot_b, d, u)


def join_kernel(g_ref, w_ref, sa_ref, sb_ref, ra_ref, rb_ref, out_ref):
    rows = g_ref.shape[0]
    slots = lax.broadcasted_iota(jnp.int32, (rows, 8 * SLOTS), 1)
    for half, (s_ref, r_ref) in enumerate(((sa_ref, ra_ref), (sb_ref, rb_ref))):
        base = lax.dot_general(
            g_ref[...], w_ref[half * HALF : (half + 1) * HALF, :], (((1,), (1,)), ((), ())),
            preferred_element_type=F32,
        )
        pick = jnp.where(slots == s_ref[...], 1.0, 0.0).astype(BF)
        base = base + jnp.dot(pick, r_ref[...].reshape(8 * SLOTS, HALF), preferred_element_type=F32)
        out_ref[:, half * HALF : (half + 1) * HALF] = base.astype(BF)


def join(g_full, w, slot_a, slot_b, ret_a, ret_b):
    rows = 256
    whole = lambda shape: pl.BlockSpec(shape, lambda i: (0,) * len(shape))
    part = lambda width: pl.BlockSpec((rows, width), lambda i: (i, 0))
    return pl.pallas_call(
        join_kernel,
        grid=(ROWS // rows,),
        out_shape=jax.ShapeDtypeStruct((ROWS, 2 * HALF), BF),
        in_specs=[
            part(1024), whole((1024, 1024)), part(1), part(1),
            whole((8, SLOTS, HALF)), whole((8, SLOTS, HALF)),
        ],
        out_specs=part(2 * HALF),
        compiler_params=pltpu.CompilerParams(vmem_limit_bytes=48 * 2**20),
        name="join",
    )(g_full, w, slot_a, slot_b, ret_a, ret_b)


def body(
    activations,
    output_gradient,
    adapter_of_row,
    frozen_value_weight,
    adapter_down_weight,
    adapter_up_weight,
):
    ids = adapter_of_row[:, 0]
    onehot = (ids[:, None] == jnp.arange(128, dtype=jnp.int32)[None, :]).astype(jnp.int32)
    position = jnp.sum(jnp.cumsum(onehot, axis=0) * onehot, axis=1) - 1
    owner, within = ids // 4, ids % 4
    core, y, x = owner % 2, (owner // 2) % 4, owner // 8
    slot_a = (y * 2 + core) * SLOTS + (x * 4 + within) * MOST + position
    slot_b = (x * 2 + core) * SLOTS + (y * 4 + within) * MOST + position
    g_full = lax.all_gather(output_gradient, "tensor", axis=1, tiled=True)
    ret_a, ret_b, down, up = rank_part(
        activations,
        output_gradient,
        slot_a[None, :],
        slot_b[None, :],
        adapter_down_weight.reshape(OWN, 2 * HALF),
        adapter_up_weight.reshape(OWN, GW),
    )
    input_gradient = join(
        g_full, frozen_value_weight, slot_a[:, None], slot_b[:, None], ret_a, ret_b
    )
    return input_gradient, down.reshape(4, RANK, 2 * HALF), up.reshape(4, RANK, GW)


def solution(mesh):
    in_specs = (
        P("adapter", "tensor"),
        P("adapter", "tensor"),
        P("adapter", None),
        P("tensor", None),
        P("adapter", None, "tensor"),
        P("adapter", None, "tensor"),
    )
    out_specs = (P("adapter", "tensor"), P("adapter", None, "tensor"), P("adapter", None, "tensor"))
    return jax.shard_map(body, mesh=mesh, in_specs=in_specs, out_specs=out_specs, check_vma=False)
```

time: 249 us -> 172 us (0.69); the launches traced: 245 us -> 171 us
  Pallas kernels: 0 us -> 142 us
  waiting for transfers between devices: 95.3 us -> 0.7 us
  local copies, waits for them, and re-layouts: 49.5 us -> 6.41 us
  blocking collectives: 42.9 us -> 0 us
  starting transfers between devices: 23.7 us -> 0.04 us
  matrix products: 16.1 us -> 0 us
  other arithmetic: 3.11 us -> 7.71 us
    pallas_call x0 -> x2, Pallas kernels: none -> 142 us  [the longest x1 128 us: rank_part(): pl.pallas_call(rank_kernel, out_shape=(jax.ShapeDtypeStruct((8, SLOTS, HA...]
    all_to_all x3 -> x0, waiting for transfers between devices: 94.8 us -> none  [the longest x1 49 us: body(): lax.all_to_all(send_rows, 'adapter', split_axis=0, concat_axis=0, tiled=T...]
    psum x1 -> x0, blocking collectives: 42.9 us -> none  [body(): lax.psum(jnp.concatenate([low_part, back_part], axis=3), 'tensor')]
    all_to_all x3 -> x0, starting transfers between devices: 23.5 us -> none  [the longest x1 8.33 us: body(): lax.all_to_all(adapter_share.reshape(owner_devices, rows_each_owner * row...]
    reshape x4 -> x0, local copies, waits for them, and re-layouts: 16.9 us -> none  [the longest x1 5.94 us: body(): send_rows.reshape(owner_devices, rows_each_owner * row_capacity, input_wi...]
    dot_general x6 -> x0, matrix products: 16.1 us -> none  [the longest x1 7.22 us: base_gradient(): lax.dot_general(lax.all_gather(output_gradient, 'tensor', axis=1, tiled=T...]
    scatter x2 -> x0, local copies, waits for them, and re-layouts: 15.6 us -> none  [the longest x1 10.7 us: body(): send_rows = jnp.zeros((adapters_all * row_capacity, input_width), jnp.bfl...]
    gather x1 -> x0, local copies, waits for them, and re-layouts: 10.4 us -> none  [body(): adapter_rows = returned_gradient[owner_slot_index]]
  transfers between devices with their start and end apart: 4 -> 1, of which waited for: 2 -> 0; matrix products, arithmetic and copies ran while one was open for 21% -> 6% of each run, Pallas kernels for 0% -> 75%
where the time goes in v1:
time: 172 us; the launch traced here: 171 us
  Pallas kernels  142 us (83%)
  between operations  14.1 us (8%)
  other arithmetic  7.71 us (4%)
  local copies, waits for them, and re-layouts  6.41 us (4%)
    pallas_call x1, Pallas kernels, rank_part(): pl.pallas_call(rank_kernel, out_shape=(jax.ShapeDtypeStruct((8, SLOTS, HA...  128 us
    pallas_call x1, Pallas kernels, join(): pl.pallas_call(join_kernel, grid=(ROWS // rows,), out_shape=jax.ShapeDtyp...  13.7 us
    unnamed x15, local copies, waits for them, and re-layouts  5.05 us
    add x2, other arithmetic, body(): slot_b = (x * 2 + core) * SLOTS + (y * 4 + within) * MOST + position  4.65 us
  transfers between devices with their start and end apart: 1, of which 0 were waited for; matrix products, arithmetic and copies ran while one was open for 6% of the time, Pallas kernels for 75%

profile of v1, /device:TPU:6, one launch (start us, length us, event | category | flops | bytes accessed | tf_op | source)
XLA Modules:
  0.0 171.1 jit_solution(16909414246550268162)
XLA Ops:
  7.2 0.0 all-gather.2.cloned.1.call-start
  7.2 0.7 all-gather.2.cloned.1.call-update
  7.9 0.7 broadcast_compare_fusion
  8.6 1.9 %copy.28 = s32[1536,1]{1,0:T(8,128)} copy(s32[1536,1]{0,1:T(1,128)} %param.8) | data formatting | bytes 12288 | tf_op args[2]
  10.5 0.8 reduce
  11.3 0.1 copy.38
  11.4 1.0 copy.33
  12.4 0.3 fusion
  12.7 0.1 broadcast_add_fusion
  12.8 0.3 copy.39
  13.1 0.5 fusion.4
  13.6 0.0 copy-done.4
  13.6 0.7 add_add_fusion
  14.3 0.6 add_add_fusion.1.sa_ref
  15.0 128.4 %rank_part.1 = (bf16[8,240,512]{2,1,0:T(8,128)(2,1)}, bf16[8,240,512]{2,1,0:T(8,128)(2,1)}, f32[256,1024]{1,0:T(8,128)}, f32[256,128]{1,0:T(8,128)}) custom-call(bf16[1536,1024]{1,0:T(8,128)(2,1)} %x_ref.1, bf16[1536,128]{1,0:T(8,128)(2,1)} %g_ref.1, s32[1,1536]{1,0:T(1,128)} %add_add_fusion.1.sa_ref, s32[1,1536]{1,0:T(1,128)} %get-tuple-element.11.sb_ref, ...), custom_call_target="tpu_custom_call" | custom-call | flops 30000001024 | bytes 20000000 | tf_op jit(solution)/shard_map/rank_part/pallas_call | solution.py:368
  143.4 0.0 copy-start
  143.4 0.0 copy-done.3
  143.4 3.9 %reshape_add_fusion = (s32[1536,1]{1,0:T(8,128)S(1)}, s32[1536,1]{1,0:T(8,128)S(1)}) fusion(s32[1536]{0:T(1024)S(1)} %broadcast_add_fusion.1, pred[1536,1]{1,0:T(8,128)(4,1)S(1)} %copy-done.3, s32[1536,1]{1,0:T(8,128)} %copy.28), kind=kLoop, calls=%fused_computation.16 | loop fusion | flops 113664 | bytes 26112 | tf_op jit(solution)/shard_map/add | solution.py:443
  147.3 0.0 all-gather.2.cloned.1.call-done.g_ref
  147.3 0.0 copy-done
  147.4 1.5 copy-done.1
  148.9 13.7 %join.1 = bf16[1536,1024]{1,0:T(8,128)(2,1)} custom-call(bf16[1536,1024]{1,0:T(8,128)(2,1)} %all-gather.2.cloned.1.call-done.g_ref, bf16[1024,1024]{1,0:T(8,128)(2,1)} %w_ref.1, s32[1536,1]{1,0:T(8,128)S(1)} %get-tuple-element.16.sa_ref, s32[1536,1]{1,0:T(8,128)S(1)} %get-tuple-element.15.sb_ref, bf16[8,240,512]{2,1,0:T(8,128)(2,1)S(1)} %copy-done, ...), custom_call_target="tpu_custom_call" | custom-call | tf_op jit(solution)/shard_map/join/pallas_call | solution.py:415
  162.6 1.0 copy.48
  163.6 0.7 copy.49
  (10 shorter events, 0.0 us)
Async XLA Ops:
  7.2 140.2 %all-gather.2.cloned.1.call-start = ((), (), s32[]{:S(2)}) async-start(), calls=%async_computation | async-start | bytes 3538944 | tf_op jit(solution)/shard_map/all_gather | solution.py:444
  10.5 3.1 %copy-start.4 = (s32[1536,1]{0,1:T(1,128)S(1)}, s32[1536,1]{0,1:T(1,128)}, u32[]{:S(2)}) copy-start(s32[1536,1]{0,1:T(1,128)} %param.8) | copy-start | bytes 18436
  15.0 128.4 %copy-start.3 = (pred[1536,1]{1,0:T(8,128)(4,1)S(1)}, pred[1536,1]{1,0:T(8,128)(4,1)}, u32[]{:S(2)}) copy-start(pred[1536,1]{1,0:T(8,128)(4,1)} %copy.33) | copy-start | bytes 4612
  143.4 4.0 %copy-start = (bf16[8,240,512]{2,1,0:T(8,128)(2,1)S(1)}, bf16[8,240,512]{2,1,0:T(8,128)(2,1)}, u32[]{:S(2)}) copy-start(bf16[8,240,512]{2,1,0:T(8,128)(2,1)} %get-tuple-element.7.ra_ref) | copy-start | bytes 5898244
  147.4 1.5 copy-start.1
  148.9 13.7 %copy-start.2 = (f32[256,1024]{1,0:T(8,128)S(1)}, f32[256,1024]{1,0:T(8,128)}, u32[]{:S(2)}) copy-start(f32[256,1024]{1,0:T(8,128)} %get-tuple-element.9) | copy-start | bytes 3145732
  148.9 14.7 %copy-start.5 = (f32[256,128]{1,0:T(8,128)S(1)}, f32[256,128]{1,0:T(8,128)}, u32[]{:S(2)}) copy-start(f32[256,128]{1,0:T(8,128)} %get-tuple-element.10) | copy-start | bytes 393220
Sparse Core Ops, SparseCore 0:
  9.7 103.4 all-gather.1

commit v2 on v1

v2 whole, which is shorter than its diff:
```python
import jax
import jax.numpy as jnp
from jax import lax
from jax.experimental import pallas as pl
from jax.experimental.pallas import tpu as pltpu
from jax.sharding import PartitionSpec as P

adapter_scale = 2.0
MESH = pl.DeviceIdType.MESH
BF = jnp.bfloat16
F32 = jnp.float32

MOST = 15
SLOTS = 240
HALF = 512
ROWS = 1536
RANK = 64
GW = 128
OWN = 256
TILE = 256

(U_A, U_B, G_A, G_B, D_A, D_B, X_A, X_B, R_A, R_B, DG_A, DG_B, UG_A, UG_B, GR, GL,
 B_RELAY, B_FINAL, B_NEAR, B_FAR, L_RELAY, L_FINAL, L_NEAR, L_FAR) = range(24)


def adapter_kernel(
    ids_ref, x_hbm, g_ref, w_hbm, d_ref, u_ref,
    out_hbm, down_ref, up_ref,
    xv, wv, sa_ref, sb_ref, cols,
    sxa, sxb, sga, sgb, rxa, rxb, rga, rgb,
    da, db, ua, ub, maskb,
    bpart, brelay, bfinal, ball, lpart, lrelay, lfinal, lall,
    ma, mb, reta, retb,
    dga, dgb, dgra, dgrb, dgo, uga, ugb, ugra, ugrb, ugo,
    gfull, acc,
    ss, rs, loc,
):
    a = lax.axis_index("adapter")
    z = lax.axis_index("tensor")
    c = a % 2
    y = (a // 2) % 4
    x = a // 8
    m_a = y * 2 + c
    m_b = x * 2 + c
    side = 2 * (z % 2) - 1

    def on_a(t):
        return ((x * 4 + t // 2) * 2 + t % 2, z)

    def on_b(t):
        return (((t // 2) * 4 + y) * 2 + t % 2, z)

    def ring_x(t):
        return ((t * 4 + y) * 2 + c, z)

    def ring_y(t):
        return ((x * 4 + t) * 2 + c, z)

    def zz(i):
        return (z + i + 16) % 8

    def on_z(i):
        return (a, zz(i))

    def copy(kind, src, dst, to, me, device):
        return pltpu.make_async_remote_copy(
            src_ref=src, dst_ref=dst, send_sem=ss.at[kind, to], recv_sem=rs.at[kind, me],
            device_id=device, device_id_type=MESH,
        )

    def arrived(kind, dst, frm):
        copy(kind, dst, dst, frm, frm, (a, z)).wait_recv()

    def left(kind, src, to):
        copy(kind, src, src, to, to, (a, z)).wait_send()

    def near_first(k):
        return jnp.where(k < 4, 2 + 4 * (k % 2) + k // 2, 4 * (1 - (k - 4) // 2) + k % 2)

    x_in = pltpu.make_async_copy(x_hbm, xv, loc.at[0])
    x_in.start()
    w_in = pltpu.make_async_copy(w_hbm, wv, loc.at[1])
    w_in.start()

    barrier = pltpu.get_barrier_semaphore()

    @pl.loop(1, 8)
    def _(d):
        pl.semaphore_signal(barrier, inc=1, device_id=on_a((m_a + d) % 8), device_id_type=MESH)
        pl.semaphore_signal(barrier, inc=1, device_id=on_z(d), device_id_type=MESH)

    @pl.loop(2, 8)
    def _(d):
        t = ((x * 2) + d) % 8
        pl.semaphore_signal(barrier, inc=1, device_id=on_b(t), device_id_type=MESH)

    with jax.named_scope("slots"):
        ids = ids_ref[...]
        hot = jnp.where(lax.broadcasted_iota(jnp.int32, (128, ROWS), 0) == ids, 1.0, 0.0)
        before = jnp.where(
            lax.broadcasted_iota(jnp.int32, (TILE, TILE), 0) < lax.broadcasted_iota(jnp.int32, (TILE, TILE), 1), 1.0, 0.0
        ).astype(BF)
        seen = jnp.zeros((128, 1), F32)
        places = []
        for q in range(ROWS // TILE):
            part = hot[:, q * TILE : (q + 1) * TILE]
            count = jnp.dot(part.astype(BF), before, preferred_element_type=F32) + seen
            places.append(jnp.sum(count * part, axis=0, keepdims=True))
            seen = seen + jnp.sum(part, axis=1, keepdims=True)
        place = jnp.concatenate(places, axis=1).astype(jnp.int32)
        owner, within = ids >> 2, ids & 3
        core, oy, ox = owner & 1, (owner >> 1) & 3, owner >> 3
        slot_a = (oy * 2 + core) * SLOTS + (ox * 4 + within) * MOST + place
        slot_b = (ox * 2 + core) * SLOTS + (oy * 4 + within) * MOST + place
        sa_ref[...] = slot_a
        sb_ref[...] = slot_b
        cols[...] = jnp.concatenate([slot_a.astype(F32), slot_b.astype(F32)] * 4, axis=0).T

        first = (lax.broadcasted_iota(jnp.int32, (SLOTS, 1024), 1) >> 6) * MOST
        row = lax.broadcasted_iota(jnp.int32, (SLOTS, 1024), 0)
        maskb[...] = jnp.where((row >= first) & (row < first + MOST), 1.0, 0.0).astype(BF)

    pl.semaphore_wait(barrier, 20)

    @pl.loop(1, 4)
    def _(d):
        tx = (x + d) % 4
        ty = (y + d) % 4
        copy(U_A, u_ref, ua.at[x], tx, x, ring_x(tx)).start()
        copy(U_B, u_ref, ub.at[y], ty, y, ring_y(ty)).start()

    ua[x] = u_ref[...]
    ub[y] = u_ref[...]

    def g_cols(i):
        return pl.ds(pl.multiple_of(zz(i) * GW, GW), GW)

    def g_whole(i):
        return gfull.at[:, g_cols(i)]

    def g_half(i, upper):
        return gfull.at[pl.ds(upper * (ROWS // 2), ROWS // 2), g_cols(i)]

    copy(GR, g_ref, g_whole(0), 0, 1, on_z(1)).start()
    copy(GL, g_ref, g_whole(0), 0, 1, on_z(-1)).start()

    def g_step(i):
        arrived(GR, g_whole(-i), i)
        arrived(GL, g_whole(i), i)
        if i < 3:
            copy(GR, g_whole(-i), g_whole(-i), i, i + 1, on_z(1)).start()
            copy(GL, g_whole(i), g_whole(i), i, i + 1, on_z(-1)).start()
        else:
            copy(GR, g_half(-i, 0), g_half(-i, 0), i, i + 1, on_z(1)).start()
            copy(GL, g_half(i, 1), g_half(i, 1), i, i + 1, on_z(-1)).start()

    slot_rows = lax.broadcasted_iota(jnp.int32, (SLOTS, ROWS), 0)

    def choose(s_ref, t):
        return jnp.where(slot_rows + t * SLOTS == s_ref[...], 1.0, 0.0).astype(BF)

    def route(kind, m, on, s_ref, value, send, recv, d):
        t = (m + d) % 8
        block = jnp.dot(choose(s_ref, t), value, preferred_element_type=F32).astype(BF)

        @pl.when(d == 0)
        def _():
            recv[m] = block

        @pl.when(d != 0)
        def _():
            send[t] = block
            copy(kind, send.at[t], recv.at[m], t, m, on(t)).start()

    with jax.named_scope("route_g"):

        @pl.loop(0, 8)
        def _(k):
            d = near_first(k)
            route(G_A, m_a, on_a, sa_ref, g_ref[...], sga, rga, d)
            route(G_B, m_b, on_b, sb_ref, g_ref[...], sgb, rgb, d)

    gfull[:, g_cols(0)] = g_ref[...]

    @pl.loop(1, 4)
    def _(d):
        tx = (x + d) % 4
        ty = (y + d) % 4
        copy(D_A, d_ref.at[:, pl.ds(0, HALF)], da.at[x], tx, x, ring_x(tx)).start()
        copy(D_B, d_ref.at[:, pl.ds(HALF, HALF)], db.at[y], ty, y, ring_y(ty)).start()

    da[x] = d_ref[:, :HALF]
    db[y] = d_ref[:, HALF:]
    x_in.wait()

    def route_x(lo, hi):
        with jax.named_scope("route_x"):

            @pl.loop(lo, hi)
            def _(k):
                d = near_first(k)
                route(X_A, m_a, on_a, sa_ref, xv[:, :HALF], sxa, rxa, d)
                route(X_B, m_b, on_b, sb_ref, xv[:, HALF:], sxb, rxb, d)

    low_lanes = lax.broadcasted_iota(jnp.int32, (SLOTS, 128), 1) < RANK

    def fold(rows, weights):
        product = lax.dot_general(rows, weights, (((1,), (1,)), ((), ())), preferred_element_type=F32)
        product = product * maskb[...].astype(F32)
        total = product[:, :128]
        for i in range(1, 8):
            total = total + product[:, i * 128 : (i + 1) * 128]
        return total + pltpu.roll(total, RANK, 1)

    def spread(both, is_a):
        wide = both.astype(F32)
        turned = pltpu.roll(wide, RANK, 1)
        one = (jnp.where(low_lanes, wide, turned) if is_a else jnp.where(low_lanes, turned, wide)).astype(BF)
        return jnp.concatenate([one] * 8, axis=1) * maskb[...]

    def over_z(relay_kind, final_kind, near_kind, far_kind, part, relay, final, everything, rows_a, weights_a, rows_b, weights_b):
        def one(i):
            t = zz(i)
            part[t] = jnp.where(
                low_lanes,
                fold(rows_a[t], weights_a[...].reshape(1024, -1)),
                fold(rows_b[t], weights_b[...].reshape(1024, -1)),
            )

        def begin():
            @pl.loop(3, 6)
            def _(i):
                one(i)

            copy(relay_kind, part.at[zz(-3)], relay.at[0], 0, 0, on_z(-1)).start()
            copy(relay_kind, part.at[zz(3)], relay.at[1], 1, 1, on_z(1)).start()
            copy(relay_kind, part.at[zz(4)], relay.at[2], 2, 2, on_z(2 * side)).start()

            @pl.loop(0, 2)
            def _(j):
                one(1 + 6 * j)

            copy(final_kind, part.at[zz(1)], final.at[0], 0, 0, on_z(1)).start()
            copy(final_kind, part.at[zz(-1)], final.at[1], 1, 1, on_z(-1)).start()

            @pl.loop(0, 3)
            def _(j):
                one(j * (j + 1))

        def pass_on():
            for i in range(3):
                arrived(relay_kind, relay.at[i], i)
            part[zz(-2)] += relay[0]
            part[zz(2)] += relay[1]
            part[zz(2 * side)] += relay[2]
            copy(final_kind, part.at[zz(2)], final.at[2], 2, 2, on_z(2)).start()
            copy(final_kind, part.at[zz(-2)], final.at[3], 3, 3, on_z(-2)).start()

        def publish():
            for i in range(4):
                arrived(final_kind, final.at[i], i)
            total = part[z] + final[0] + final[1] + final[2] + final[3]
            everything[z] = total.astype(BF)
            for i, step in enumerate((1, -1, 2, -2)):
                copy(near_kind, everything.at[z], everything.at[z], i, i, on_z(step)).start()

        def forward():
            arrived(near_kind, everything.at[zz(-2)], 2)
            arrived(near_kind, everything.at[zz(2)], 3)
            for i, (chunk, step) in enumerate(((-2, 1), (2, -1), (2 * side, -2 * side))):
                copy(far_kind, everything.at[zz(chunk)], everything.at[zz(chunk)], i, i, on_z(step)).start()

        def collect():
            arrived(near_kind, everything.at[zz(-1)], 0)
            arrived(near_kind, everything.at[zz(1)], 1)
            arrived(far_kind, everything.at[zz(-3)], 0)
            arrived(far_kind, everything.at[zz(3)], 1)
            arrived(far_kind, everything.at[zz(4)], 2)

        def finish():
            left(relay_kind, part.at[zz(-3)], 0)
            left(relay_kind, part.at[zz(3)], 1)
            left(relay_kind, part.at[zz(4)], 2)
            left(final_kind, part.at[zz(1)], 0)
            left(final_kind, part.at[zz(-1)], 1)
            left(final_kind, part.at[zz(2)], 2)
            left(final_kind, part.at[zz(-2)], 3)
            for i in range(4):
                left(near_kind, everything.at[z], i)
            for i in range(3):
                left(far_kind, everything.at[z], i)

        return begin, pass_on, publish, forward, collect, finish

    back = over_z(B_RELAY, B_FINAL, B_NEAR, B_FAR, bpart, brelay, bfinal, ball, rga, ua, rgb, ub)
    low = over_z(L_RELAY, L_FINAL, L_NEAR, L_FAR, lpart, lrelay, lfinal, lall, rxa, da, rxb, db)

    route_x(0, 4)

    with jax.named_scope("back_parts"):

        @pl.loop(1, 4)
        def _(d):
            fx = (x + d) % 4
            fy = (y + d) % 4
            arrived(U_A, ua.at[fx], fx)
            arrived(U_B, ub.at[fy], fy)

        @pl.loop(1, 8)
        def _(d):
            fa = (m_a + d) % 8
            fb = (m_b + d) % 8
            arrived(G_A, rga.at[fa], fa)
            arrived(G_B, rgb.at[fb], fb)

        back[0]()

    route_x(4, 8)
    with jax.named_scope("g_step_1"):
        g_step(1)
    with jax.named_scope("back_pass_on"):
        back[1]()
    with jax.named_scope("back_publish"):
        back[2]()
    with jax.named_scope("g_step_2"):
        g_step(2)
    with jax.named_scope("back_forward"):
        back[3]()
    with jax.named_scope("back_collect"):
        back[4]()

    with jax.named_scope("wait_d"):

        @pl.loop(1, 4)
        def _(d):
            fx = (x + d) % 4
            fy = (y + d) % 4
            arrived(D_A, da.at[fx], fx)
            arrived(D_B, db.at[fy], fy)

    def give_back(x_kind, kind, m, on, masked, is_a, weights, out, ret, d):
        s = (m + d) % 8
        block = spread(ball[s], is_a)
        masked[s] = block
        value = (
            adapter_scale * jnp.dot(block, weights[...].reshape(1024, HALF), preferred_element_type=F32)
        ).astype(BF)

        @pl.when(d != 0)
        def _():
            left(x_kind, out.at[s], s)
            out[s] = value
            copy(kind, out.at[s], ret.at[m], s, m, on(s)).start()

        @pl.when(d == 0)
        def _():
            ret[m] = value

    def give_back_all(lo, hi):
        with jax.named_scope("give_back"):

            @pl.loop(lo, hi)
            def _(k):
                d = near_first(k)
                give_back(X_A, R_A, m_a, on_a, ma, True, da, sxa, reta, d)
                give_back(X_B, R_B, m_b, on_b, mb, False, db, sxb, retb, d)

    give_back_all(0, 4)
    with jax.named_scope("g_step_3"):
        g_step(3)
    give_back_all(4, 8)

    with jax.named_scope("wait_x"):

        @pl.loop(1, 8)
        def _(d):
            fa = (m_a + d) % 8
            fb = (m_b + d) % 8
            arrived(X_A, rxa.at[fa], fa)
            arrived(X_B, rxb.at[fb], fb)

    with jax.named_scope("low_parts"):
        low[0]()

    def gradient(masked, rows, q):
        return adapter_scale * lax.dot_general(
            masked[:, :, pl.ds(pl.multiple_of(q * OWN, OWN), OWN)].reshape(8 * SLOTS, OWN),
            rows[...].reshape(8 * SLOTS, -1),
            (((0,), (0,)), ((), ())),
            preferred_element_type=F32,
        )

    def to_owner(kind, m, ring, masked, rows, part, recv, own, half, d):
        q = (m + d) % 4
        value = gradient(masked, rows, q)

        @pl.when(d == 4)
        def _():
            own[half] = value

        @pl.when(d != 4)
        def _():
            part[q] = value.astype(part.dtype)
            copy(kind, part.at[q], recv.at[m], q, m, ring(q)).start()

    with jax.named_scope("down_gradient"):

        @pl.loop(1, 5)
        def _(d):
            to_owner(DG_A, x, ring_x, ma, rxa, dga, dgra, dgo, 0, d)
            to_owner(DG_B, y, ring_y, mb, rxb, dgb, dgrb, dgo, 1, d)

    with jax.named_scope("low_pass_on"):
        low[1]()

    with jax.named_scope("frozen"):
        arrived(GR, g_half(-4, 0), 4)
        arrived(GL, g_half(4, 1), 4)
        w_in.wait()

        @pl.loop(0, ROWS // TILE)
        def _(i):
            rows = pl.ds(pl.multiple_of(i * TILE, TILE), TILE)
            acc[rows, :] = lax.dot_general(
                gfull[rows, :], wv[...], (((1,), (1,)), ((), ())), preferred_element_type=F32
            )

    with jax.named_scope("low_publish"):
        low[2]()

    lanes = lax.broadcasted_iota(jnp.int32, (TILE, SLOTS), 1)

    def take(pair_number, last):
        with jax.named_scope("take_back"):
            blocks = []
            for j in range(2):
                d = near_first(jnp.int32(2 * pair_number + j))
                ta = (m_a - d + 8) % 8
                tb = (m_b - d + 8) % 8

                @pl.when(d != 0)
                def _():
                    arrived(R_A, reta.at[ta], ta)
                    arrived(R_B, retb.at[tb], tb)

                blocks.append((ta, tb))

            @pl.loop(0, ROWS // TILE)
            def _(i):
                rows = pl.ds(pl.multiple_of(i * TILE, TILE), TILE)
                slots = cols[rows, :].astype(jnp.int32)
                for half, ret in enumerate((reta, retb)):
                    here = pl.ds(half * HALF, HALF)
                    total = acc[rows, here]
                    for ts in blocks:
                        t = ts[half]
                        pick = jnp.where(lanes + t * SLOTS == slots[:, half : half + 1], 1.0, 0.0).astype(BF)
                        total = total + jnp.dot(pick, ret[t], preferred_element_type=F32)
                    if last:
                        xv[rows, here] = total.astype(BF)
                    else:
                        acc[rows, here] = total
                if last:
                    pltpu.make_async_copy(xv.at[rows, :], out_hbm.at[rows, :], loc.at[2 + i]).start()

    take(0, False)
    with jax.named_scope("low_forward"):
        low[3]()
    take(1, False)

    with jax.named_scope("up_gradient"):
        low[4]()

        @pl.loop(0, 8)
        def _(s):
            ma[s] = spread(lall[s], True)
            mb[s] = spread(lall[s], False)

        @pl.loop(1, 5)
        def _(d):
            to_owner(UG_A, x, ring_x, ma, rga, uga, ugra, ugo, 0, d)
            to_owner(UG_B, y, ring_y, mb, rgb, ugb, ugrb, ugo, 1, d)

    take(2, False)
    take(3, True)

    with jax.named_scope("down_sum"):

        @pl.loop(1, 4)
        def _(d):
            fx = (x + d) % 4
            fy = (y + d) % 4
            arrived(DG_A, dgra.at[fx], fx)
            arrived(DG_B, dgrb.at[fy], fy)
            dgo[0] += dgra[fx].astype(F32)
            dgo[1] += dgrb[fy].astype(F32)

        down_ref[:, :HALF] = dgo[0]
        down_ref[:, HALF:] = dgo[1]

    with jax.named_scope("up_sum"):

        @pl.loop(1, 4)
        def _(d):
            fx = (x + d) % 4
            fy = (y + d) % 4
            arrived(UG_A, ugra.at[fx], fx)
            arrived(UG_B, ugrb.at[fy], fy)
            ugo[0] += ugra[fx]
            ugo[1] += ugrb[fy]

        up_ref[...] = ugo[0] + ugo[1]

    @pl.loop(1, 8)
    def _(d):
        ta = (m_a + d) % 8
        tb = (m_b + d) % 8
        left(G_A, sga.at[ta], ta)
        left(G_B, sgb.at[tb], tb)
        left(R_A, sxa.at[ta], ta)
        left(R_B, sxb.at[tb], tb)

    @pl.loop(1, 4)
    def _(d):
        tx = (x + d) % 4
        ty = (y + d) % 4
        left(U_A, u_ref, tx)
        left(U_B, u_ref, ty)
        left(D_A, d_ref.at[:, pl.ds(0, HALF)], tx)
        left(D_B, d_ref.at[:, pl.ds(HALF, HALF)], ty)
        left(DG_A, dga.at[tx], tx)
        left(DG_B, dgb.at[ty], ty)
        left(UG_A, uga.at[tx], tx)
        left(UG_B, ugb.at[ty], ty)

    back[5]()
    low[5]()
    left(GR, g_ref, 0)
    left(GL, g_ref, 0)
    for i in (1, 2):
        left(GR, g_whole(-i), i)
        left(GL, g_whole(i), i)
    left(GR, g_half(-3, 0), 3)
    left(GL, g_half(3, 1), 3)

    @pl.loop(0, ROWS // TILE)
    def _(i):
        rows = pl.ds(pl.multiple_of(i * TILE, TILE), TILE)
        pltpu.make_async_copy(xv.at[rows, :], out_hbm.at[rows, :], loc.at[2 + i]).wait()


def adapter_backward(ids, x, g, w, d, u):
    vmem = pl.BlockSpec(memory_space=pltpu.VMEM)
    hbm = pl.BlockSpec(memory_space=pl.ANY)

    def blocks(count, width, dtype=BF):
        return pltpu.VMEM((count, SLOTS, width), dtype)

    def chunk(width, dtype=BF):
        return pltpu.VMEM((4, OWN, width), dtype)

    sums = [blocks(8, 128, F32), blocks(3, 128, F32), blocks(4, 128, F32), blocks(8, 128)]
    return pl.pallas_call(
        adapter_kernel,
        out_shape=(
            jax.ShapeDtypeStruct((ROWS, 2 * HALF), BF),
            jax.ShapeDtypeStruct((OWN, 2 * HALF), F32),
            jax.ShapeDtypeStruct((OWN, GW), F32),
        ),
        in_specs=[vmem, hbm, vmem, hbm, vmem, vmem],
        out_specs=(hbm, vmem, vmem),
        scratch_shapes=[
            pltpu.VMEM((ROWS, 2 * HALF), BF), pltpu.VMEM((2 * HALF, 1024), BF),
            pltpu.VMEM((1, ROWS), jnp.int32), pltpu.VMEM((1, ROWS), jnp.int32), pltpu.VMEM((ROWS, 8), F32),
            blocks(8, HALF), blocks(8, HALF), blocks(8, GW), blocks(8, GW),
            blocks(8, HALF), blocks(8, HALF), blocks(8, GW), blocks(8, GW),
            chunk(HALF), chunk(HALF), chunk(GW), chunk(GW), pltpu.VMEM((SLOTS, 1024), BF),
            *sums, *sums,
            blocks(8, 1024), blocks(8, 1024), blocks(8, HALF), blocks(8, HALF),
            chunk(HALF), chunk(HALF), chunk(HALF), chunk(HALF), pltpu.VMEM((2, OWN, HALF), F32),
            chunk(GW, F32), chunk(GW, F32), chunk(GW, F32), chunk(GW, F32), pltpu.VMEM((2, OWN, GW), F32),
            pltpu.VMEM((ROWS, 1024), BF), pltpu.VMEM((ROWS, 2 * HALF), F32),
            pltpu.SemaphoreType.DMA((24, 8)), pltpu.SemaphoreType.DMA((24, 8)), pltpu.SemaphoreType.DMA((8,)),
        ],
        compiler_params=pltpu.CompilerParams(
            collective_id=0, has_side_effects=True, vmem_limit_bytes=62 * 2**20
        ),
        cost_estimate=pl.CostEstimate(flops=32 * 10**9, bytes_accessed=12 * 10**6, transcendentals=0),
        name="adapter_backward",
    )(ids, x, g, w, d, u)


def body(
    activations,
    output_gradient,
    adapter_of_row,
    frozen_value_weight,
    adapter_down_weight,
    adapter_up_weight,
):
    input_gradient, down, up = adapter_backward(
        adapter_of_row.reshape(1, ROWS),
        activations,
        output_gradient,
        frozen_value_weight,
        adapter_down_weight.reshape(OWN, 2 * HALF),
        adapter_up_weight.reshape(OWN, GW),
    )
    return input_gradient, down.reshape(4, RANK, 2 * HALF), up.reshape(4, RANK, GW)


def solution(mesh):
    in_specs = (
        P("adapter", "tensor"),
        P("adapter", "tensor"),
        P("adapter", None),
        P("tensor", None),
        P("adapter", None, "tensor"),
        P("adapter", None, "tensor"),
    )
    out_specs = (P("adapter", "tensor"), P("adapter", None, "tensor"), P("adapter", None, "tensor"))
    return jax.shard_map(body, mesh=mesh, in_specs=in_specs, out_specs=out_specs, check_vma=False)
```

time: 172 us -> 128 us (0.74)
  Pallas kernels: 142 us -> 122 us
  between operations: 14.1 us -> 0.66 us
  other arithmetic: 7.71 us -> 0 us
    pallas_call x2 -> x1, Pallas kernels: 142 us -> 122 us  [adapter_backward(): pl.pallas_call(adapter_kernel, out_shape=(jax.ShapeDtypeStruct((ROWS, 2 *...]
    add x3 -> x0, other arithmetic: 5.29 us -> none  [the longest x2 4.65 us: body(): slot_b = (x * 2 + core) * SLOTS + (y * 4 + within) * MOST + position]
    unnamed x15 -> x7, local copies, waits for them, and re-layouts: 5.05 us -> 5.59 us
  transfers between devices with their start and end apart: 1 -> 0, of which waited for: 0 -> 0; matrix products, arithmetic and copies ran while one was open for 6% -> 0% of each run, Pallas kernels for 75% -> 0%
where the time goes in v2:
time: 128 us
  Pallas kernels  122 us (95%)
  local copies, waits for them, and re-layouts  5.59 us (4%)
    pallas_call x1, Pallas kernels, adapter_backward(): pl.pallas_call(adapter_kernel, out_shape=(jax.ShapeDtypeStruct((ROWS, 2 *...  122 us
    unnamed x7, local copies, waits for them, and re-layouts  5.59 us

profile of v2, /device:TPU:6, one launch (start us, length us, event | category | flops | bytes accessed | tf_op | source)
XLA Modules:
  0.0 128.1 jit_solution(1365535649678401935)
XLA Ops:
  0.6 121.8 %adapter_backward.1 = (bf16[1536,1024]{1,0:T(8,128)(2,1)}, f32[256,1024]{1,0:T(8,128)}, f32[256,128]{1,0:T(8,128)}) custom-call(s32[1,1536]{1,0:T(1,128)} %bitcast.9, bf16[1536,1024]{1,0:T(8,128)(2,1)} %x_hbm.1, bf16[1536,128]{1,0:T(8,128)(2,1)} %g_ref.1, bf16[1024,1024]{1,0:T(8,128)(2,1)} %w_hbm.1, bf16[256,1024]{1,0:T(8,128)(2,1)} %bitcast.7, ...), custom_call_target="tpu_custom_call" | custom-call | flops 32000000000 | bytes 12000000 | tf_op jit(solution)/shard_map/adapter_backward/pallas_call | solution.py:563
  122.5 0.0 copy-start
  122.5 0.0 copy-start.1
  122.5 4.0 %copy.12 = bf16[1536,1024]{1,0:T(8,128)(2,1)} copy(bf16[1536,1024]{1,0:T(8,128)(2,1)} %get-tuple-element.12) | data formatting | bytes 6291456
  126.4 0.0 copy-done
  126.4 1.0 copy.13
  127.4 0.0 copy-done.1
  127.4 0.7 copy.14
Async XLA Ops:
  122.5 4.0 %copy-start = (f32[256,1024]{1,0:T(8,128)S(1)}, f32[256,1024]{1,0:T(8,128)}, u32[]{:S(2)}) copy-start(f32[256,1024]{1,0:T(8,128)} %get-tuple-element.7) | copy-start | bytes 3145732
  122.5 4.9 %copy-start.1 = (f32[256,128]{1,0:T(8,128)S(1)}, f32[256,128]{1,0:T(8,128)}, u32[]{:S(2)}) copy-start(f32[256,128]{1,0:T(8,128)} %get-tuple-element.8) | copy-start | bytes 393220

commit v3 on v2

--- a/solution.py
+++ b/solution.py
@@ -20,7 +20,7 @@
 TILE = 256
 
 (U_A, U_B, G_A, G_B, D_A, D_B, X_A, X_B, R_A, R_B, DG_A, DG_B, UG_A, UG_B, GR, GL,
- B_RELAY, B_FINAL, B_NEAR, B_FAR, L_RELAY, L_FINAL, L_NEAR, L_FAR) = range(24)
+ B_RELAY, B_FINAL, B_NEAR, B_FAR, L_RELAY, L_FINAL, L_NEAR, L_FAR, FU_A, FU_B, FD_A, FD_B) = range(28)
 
 
 def adapter_kernel(
@@ -122,13 +122,32 @@
 
     pl.semaphore_wait(barrier, 20)
 
-    @pl.loop(1, 4)
-    def _(d):
-        tx = (x + d) % 4
-        ty = (y + d) % 4
-        copy(U_A, u_ref, ua.at[x], tx, x, ring_x(tx)).start()
-        copy(U_B, u_ref, ub.at[y], ty, y, ring_y(ty)).start()
-
+    def spread_ring(kind_a, kind_b, src_a, src_b, dst_a, dst_b):
+        for d in (1, 3):
+            tx = (x + d) % 4
+            ty = (y + d) % 4
+            copy(kind_a, src_a, dst_a.at[x], tx, x, ring_x(tx)).start()
+            copy(kind_b, src_b, dst_b.at[y], ty, y, ring_y(ty)).start()
+
+    def upper(ref, t):
+        return ref.at[t, pl.ds(0, OWN // 2), :]
+
+    def lower(ref, t):
+        return ref.at[t, pl.ds(OWN // 2, OWN // 2), :]
+
+    def forward_ring(kind, far_kind, dst, m, ring):
+        before, after = (m + 3) % 4, (m + 1) % 4
+        arrived(kind, dst.at[before], before)
+        arrived(kind, dst.at[after], after)
+        copy(far_kind, upper(dst, before), upper(dst, before), 0, 0, ring(after)).start()
+        copy(far_kind, lower(dst, after), lower(dst, after), 1, 1, ring(before)).start()
+
+    def opposite_ring(far_kind, dst, m):
+        across = (m + 2) % 4
+        arrived(far_kind, upper(dst, across), 0)
+        arrived(far_kind, lower(dst, across), 1)
+
+    spread_ring(U_A, U_B, u_ref, u_ref, ua, ub)
     ua[x] = u_ref[...]
     ub[y] = u_ref[...]
 
@@ -159,7 +178,7 @@
     def choose(s_ref, t):
         return jnp.where(slot_rows + t * SLOTS == s_ref[...], 1.0, 0.0).astype(BF)
 
-    def route(kind, m, on, s_ref, value, send, recv, d):
+    def route(kind, m, on, s_ref, value, send, recv, d, hold=False):
         t = (m + d) % 8
         block = jnp.dot(choose(s_ref, t), value, preferred_element_type=F32).astype(BF)
 
@@ -170,7 +189,8 @@
         @pl.when(d != 0)
         def _():
             send[t] = block
-            copy(kind, send.at[t], recv.at[m], t, m, on(t)).start()
+            if not hold:
+                copy(kind, send.at[t], recv.at[m], t, m, on(t)).start()
 
     with jax.named_scope("route_g"):
 
@@ -182,25 +202,30 @@
 
     gfull[:, g_cols(0)] = g_ref[...]
 
-    @pl.loop(1, 4)
-    def _(d):
-        tx = (x + d) % 4
-        ty = (y + d) % 4
-        copy(D_A, d_ref.at[:, pl.ds(0, HALF)], da.at[x], tx, x, ring_x(tx)).start()
-        copy(D_B, d_ref.at[:, pl.ds(HALF, HALF)], db.at[y], ty, y, ring_y(ty)).start()
-
+    spread_ring(D_A, D_B, d_ref.at[:, pl.ds(0, HALF)], d_ref.at[:, pl.ds(HALF, HALF)], da, db)
+    forward_ring(U_A, FU_A, ua, x, ring_x)
+    forward_ring(U_B, FU_B, ub, y, ring_y)
     da[x] = d_ref[:, :HALF]
     db[y] = d_ref[:, HALF:]
     x_in.wait()
 
-    def route_x(lo, hi):
+    def route_x(lo, hi, hold=False):
         with jax.named_scope("route_x"):
 
             @pl.loop(lo, hi)
             def _(k):
                 d = near_first(k)
-                route(X_A, m_a, on_a, sa_ref, xv[:, :HALF], sxa, rxa, d)
-                route(X_B, m_b, on_b, sb_ref, xv[:, HALF:], sxb, rxb, d)
+                route(X_A, m_a, on_a, sa_ref, xv[:, :HALF], sxa, rxa, d, hold)
+                route(X_B, m_b, on_b, sb_ref, xv[:, HALF:], sxb, rxb, d, hold)
+
+    def release_x(lo, hi):
+        @pl.loop(lo, hi)
+        def _(k):
+            d = near_first(k)
+            ta = (m_a + d) % 8
+            tb = (m_b + d) % 8
+            copy(X_A, sxa.at[ta], rxa.at[m_a], ta, m_a, on_a(ta)).start()
+            copy(X_B, sxb.at[tb], rxb.at[m_b], tb, m_b, on_b(tb)).start()
 
     low_lanes = lax.broadcasted_iota(jnp.int32, (SLOTS, 128), 1) < RANK
 
@@ -295,48 +320,31 @@
     back = over_z(B_RELAY, B_FINAL, B_NEAR, B_FAR, bpart, brelay, bfinal, ball, rga, ua, rgb, ub)
     low = over_z(L_RELAY, L_FINAL, L_NEAR, L_FAR, lpart, lrelay, lfinal, lall, rxa, da, rxb, db)
 
-    route_x(0, 4)
-
-    with jax.named_scope("back_parts"):
-
-        @pl.loop(1, 4)
-        def _(d):
-            fx = (x + d) % 4
-            fy = (y + d) % 4
-            arrived(U_A, ua.at[fx], fx)
-            arrived(U_B, ub.at[fy], fy)
-
-        @pl.loop(1, 8)
-        def _(d):
-            fa = (m_a + d) % 8
-            fb = (m_b + d) % 8
-            arrived(G_A, rga.at[fa], fa)
-            arrived(G_B, rgb.at[fb], fb)
-
-        back[0]()
-
-    route_x(4, 8)
-    with jax.named_scope("g_step_1"):
-        g_step(1)
-    with jax.named_scope("back_pass_on"):
-        back[1]()
-    with jax.named_scope("back_publish"):
-        back[2]()
-    with jax.named_scope("g_step_2"):
-        g_step(2)
-    with jax.named_scope("back_forward"):
-        back[3]()
-    with jax.named_scope("back_collect"):
-        back[4]()
-
-    with jax.named_scope("wait_d"):
-
-        @pl.loop(1, 4)
-        def _(d):
-            fx = (x + d) % 4
-            fy = (y + d) % 4
-            arrived(D_A, da.at[fx], fx)
-            arrived(D_B, db.at[fy], fy)
+    route_x(0, 2, hold=True)
+    opposite_ring(FU_A, ua, x)
+    opposite_ring(FU_B, ub, y)
+
+    @pl.loop(1, 8)
+    def _(d):
+        fa = (m_a + d) % 8
+        fb = (m_b + d) % 8
+        arrived(G_A, rga.at[fa], fa)
+        arrived(G_B, rgb.at[fb], fb)
+
+    release_x(0, 2)
+    back[0]()
+    route_x(2, 4)
+    back[1]()
+    route_x(4, 6)
+    back[2]()
+    route_x(6, 8)
+    back[3]()
+    forward_ring(D_A, FD_A, da, x, ring_x)
+    forward_ring(D_B, FD_B, db, y, ring_y)
+    back[4]()
+    g_step(1)
+    opposite_ring(FD_A, da, x)
+    opposite_ring(FD_B, db, y)
 
     def give_back(x_kind, kind, m, on, masked, is_a, weights, out, ret, d):
         s = (m + d) % 8
@@ -365,10 +373,8 @@
                 give_back(X_A, R_A, m_a, on_a, ma, True, da, sxa, reta, d)
                 give_back(X_B, R_B, m_b, on_b, mb, False, db, sxb, retb, d)
 
-    give_back_all(0, 4)
-    with jax.named_scope("g_step_3"):
-        g_step(3)
-    give_back_all(4, 8)
+    give_back_all(0, 8)
+    g_step(2)
 
     with jax.named_scope("wait_x"):
 
@@ -390,28 +396,45 @@
             preferred_element_type=F32,
         )
 
-    def to_owner(kind, m, ring, masked, rows, part, recv, own, half, d):
-        q = (m + d) % 4
-        value = gradient(masked, rows, q)
-
-        @pl.when(d == 4)
-        def _():
-            own[half] = value
-
-        @pl.when(d != 4)
-        def _():
-            part[q] = value.astype(part.dtype)
-            copy(kind, part.at[q], recv.at[m], q, m, ring(q)).start()
-
-    with jax.named_scope("down_gradient"):
-
-        @pl.loop(1, 5)
-        def _(d):
-            to_owner(DG_A, x, ring_x, ma, rxa, dga, dgra, dgo, 0, d)
-            to_owner(DG_B, y, ring_y, mb, rxb, dgb, dgrb, dgo, 1, d)
-
-    with jax.named_scope("low_pass_on"):
-        low[1]()
+    def to_owners(kind, m, ring, masked, rows, part, recv, own, half, first):
+        across, after, before = (m + 2) % 4, (m + 1) % 4, (m + 3) % 4
+        if first:
+            part[across] = gradient(masked, rows, across).astype(part.dtype)
+            copy(kind, upper(part, across), upper(recv, 2), 2, 2, ring(after)).start()
+            copy(kind, lower(part, across), lower(recv, 2), 3, 3, ring(before)).start()
+            own[half] = gradient(masked, rows, m)
+        else:
+            for t, slot, edge, at in ((after, 0, upper, 0), (before, 1, lower, OWN // 2)):
+                value = gradient(masked, rows, t)
+                arrived(kind, edge(recv, 2), 2 + slot)
+                part[t] = value.astype(part.dtype)
+                rows_of = pl.ds(at, OWN // 2)
+                part[t, rows_of, :] = (
+                    value[at : at + OWN // 2] + recv[2, rows_of, :].astype(F32)
+                ).astype(part.dtype)
+                copy(kind, part.at[t], recv.at[slot], slot, slot, ring(t)).start()
+
+    def from_neighbours(kind, recv, own, half):
+        for slot in range(2):
+            arrived(kind, recv.at[slot], slot)
+        own[half] += recv[0].astype(F32) + recv[1].astype(F32)
+
+    def sent_to_owners(kind, m, part):
+        across = (m + 2) % 4
+        left(kind, part.at[0], 0)
+        left(kind, part.at[0], 1)
+        left(kind, upper(part, across), 2)
+        left(kind, lower(part, across), 3)
+
+    def down_gradient(first):
+        with jax.named_scope("down_gradient"):
+            to_owners(DG_A, x, ring_x, ma, rxa, dga, dgra, dgo, 0, first)
+            to_owners(DG_B, y, ring_y, mb, rxb, dgb, dgrb, dgo, 1, first)
+
+    low[1]()
+    down_gradient(True)
+    g_step(3)
+    low[2]()
 
     with jax.named_scope("frozen"):
         arrived(GR, g_half(-4, 0), 4)
@@ -425,8 +448,7 @@
                 gfull[rows, :], wv[...], (((1,), (1,)), ((), ())), preferred_element_type=F32
             )
 
-    with jax.named_scope("low_publish"):
-        low[2]()
+    low[3]()
 
     lanes = lax.broadcasted_iota(jnp.int32, (TILE, SLOTS), 1)
 
@@ -463,13 +485,27 @@
                 if last:
                     pltpu.make_async_copy(xv.at[rows, :], out_hbm.at[rows, :], loc.at[2 + i]).start()
 
+    def to_owner(kind, m, ring, masked, rows, part, recv, own, half, d):
+        q = (m + d) % 4
+        value = gradient(masked, rows, q)
+
+        @pl.when(d == 4)
+        def _():
+            own[half] = value
+
+        @pl.when(d != 4)
+        def _():
+            part[q] = value
+            copy(kind, part.at[q], recv.at[m], q, m, ring(q)).start()
+
     take(0, False)
-    with jax.named_scope("low_forward"):
-        low[3]()
     take(1, False)
+    down_gradient(False)
+    take(2, False)
+    take(3, True)
+    low[4]()
 
     with jax.named_scope("up_gradient"):
-        low[4]()
 
         @pl.loop(0, 8)
         def _(s):
@@ -481,20 +517,9 @@
             to_owner(UG_A, x, ring_x, ma, rga, uga, ugra, ugo, 0, d)
             to_owner(UG_B, y, ring_y, mb, rgb, ugb, ugrb, ugo, 1, d)
 
-    take(2, False)
-    take(3, True)
-
     with jax.named_scope("down_sum"):
-
-        @pl.loop(1, 4)
-        def _(d):
-            fx = (x + d) % 4
-            fy = (y + d) % 4
-            arrived(DG_A, dgra.at[fx], fx)
-            arrived(DG_B, dgrb.at[fy], fy)
-            dgo[0] += dgra[fx].astype(F32)
-            dgo[1] += dgrb[fy].astype(F32)
-
+        from_neighbours(DG_A, dgra, dgo, 0)
+        from_neighbours(DG_B, dgrb, dgo, 1)
         down_ref[:, :HALF] = dgo[0]
         down_ref[:, HALF:] = dgo[1]
 
@@ -520,18 +545,26 @@
         left(R_A, sxa.at[ta], ta)
         left(R_B, sxb.at[tb], tb)
 
-    @pl.loop(1, 4)
-    def _(d):
+    for d in (1, 3):
         tx = (x + d) % 4
         ty = (y + d) % 4
         left(U_A, u_ref, tx)
         left(U_B, u_ref, ty)
         left(D_A, d_ref.at[:, pl.ds(0, HALF)], tx)
         left(D_B, d_ref.at[:, pl.ds(HALF, HALF)], ty)
-        left(DG_A, dga.at[tx], tx)
-        left(DG_B, dgb.at[ty], ty)
-        left(UG_A, uga.at[tx], tx)
-        left(UG_B, ugb.at[ty], ty)
+    for i in range(2):
+        left(FU_A, upper(ua, 0), i)
+        left(FU_B, upper(ub, 0), i)
+        left(FD_A, upper(da, 0), i)
+        left(FD_B, upper(db, 0), i)
+    sent_to_owners(DG_A, x, dga)
+    sent_to_owners(DG_B, y, dgb)
+
+    @pl.loop(1, 4)
+    def _(d):
+        left(UG_A, uga.at[(x + d) % 4], (x + d) % 4)
+        left(UG_B, ugb.at[(y + d) % 4], (y + d) % 4)
+
 
     back[5]()
     low[5]()
@@ -580,7 +613,7 @@
             chunk(HALF), chunk(HALF), chunk(HALF), chunk(HALF), pltpu.VMEM((2, OWN, HALF), F32),
             chunk(GW, F32), chunk(GW, F32), chunk(GW, F32), chunk(GW, F32), pltpu.VMEM((2, OWN, GW), F32),
             pltpu.VMEM((ROWS, 1024), BF), pltpu.VMEM((ROWS, 2 * HALF), F32),
-            pltpu.SemaphoreType.DMA((24, 8)), pltpu.SemaphoreType.DMA((24, 8)), pltpu.SemaphoreType.DMA((8,)),
+            pltpu.SemaphoreType.DMA((28, 8)), pltpu.SemaphoreType.DMA((28, 8)), pltpu.SemaphoreType.DMA((8,)),
         ],
         compiler_params=pltpu.CompilerParams(
             collective_id=0, has_side_effects=True, vmem_limit_bytes=62 * 2**20

time: 128 us -> 132 us (1.031); the launches traced: 128 us -> 130 us
  Pallas kernels: 122 us -> 124 us
    pallas_call x1, Pallas kernels: 122 us -> 124 us  [adapter_backward(): pl.pallas_call(adapter_kernel, out_shape=(jax.ShapeDtypeStruct((ROWS, 2 *...]
where the time goes in v3:
time: 132 us; the launch traced here: 130 us
  Pallas kernels  124 us (94%)
  local copies, waits for them, and re-layouts  5.59 us (4%)
    pallas_call x1, Pallas kernels, adapter_backward(): pl.pallas_call(adapter_kernel, out_shape=(jax.ShapeDtypeStruct((ROWS, 2 *...  124 us
    unnamed x7, local copies, waits for them, and re-layouts  5.59 us

profile of v3, /device:TPU:6, one launch (start us, length us, event | category | flops | bytes accessed | tf_op | source)
XLA Modules:
  0.0 129.8 jit_solution(13225052631658744320)
XLA Ops:
  0.6 123.6 %adapter_backward.1 = (bf16[1536,1024]{1,0:T(8,128)(2,1)}, f32[256,1024]{1,0:T(8,128)}, f32[256,128]{1,0:T(8,128)}) custom-call(s32[1,1536]{1,0:T(1,128)} %bitcast.9, bf16[1536,1024]{1,0:T(8,128)(2,1)} %x_hbm.1, bf16[1536,128]{1,0:T(8,128)(2,1)} %g_ref.1, bf16[1024,1024]{1,0:T(8,128)(2,1)} %w_hbm.1, bf16[256,1024]{1,0:T(8,128)(2,1)} %bitcast.7, ...), custom_call_target="tpu_custom_call" | custom-call | flops 32000000000 | bytes 12000000 | tf_op jit(solution)/shard_map/adapter_backward/pallas_call | solution.py:596
  124.2 0.0 copy-start
  124.2 0.0 copy-start.1
  124.2 4.0 %copy.12 = bf16[1536,1024]{1,0:T(8,128)(2,1)} copy(bf16[1536,1024]{1,0:T(8,128)(2,1)} %get-tuple-element.12) | data formatting | bytes 6291456
  128.2 0.0 copy-done
  128.2 1.0 copy.13
  129.2 0.0 copy-done.1
  129.2 0.7 copy.14
Async XLA Ops:
  124.2 4.0 %copy-start = (f32[256,1024]{1,0:T(8,128)S(1)}, f32[256,1024]{1,0:T(8,128)}, u32[]{:S(2)}) copy-start(f32[256,1024]{1,0:T(8,128)} %get-tuple-element.7) | copy-start | bytes 3145732
  124.2 4.9 %copy-start.1 = (f32[256,128]{1,0:T(8,128)S(1)}, f32[256,128]{1,0:T(8,128)}, u32[]{:S(2)}) copy-start(f32[256,128]{1,0:T(8,128)} %get-tuple-element.8) | copy-start | bytes 393220

commit v4 on v3

--- a/solution.py
+++ b/solution.py
@@ -202,7 +202,6 @@
 
     gfull[:, g_cols(0)] = g_ref[...]
 
-    spread_ring(D_A, D_B, d_ref.at[:, pl.ds(0, HALF)], d_ref.at[:, pl.ds(HALF, HALF)], da, db)
     forward_ring(U_A, FU_A, ua, x, ring_x)
     forward_ring(U_B, FU_B, ub, y, ring_y)
     da[x] = d_ref[:, :HALF]
@@ -261,6 +260,7 @@
             copy(relay_kind, part.at[zz(3)], relay.at[1], 1, 1, on_z(1)).start()
             copy(relay_kind, part.at[zz(4)], relay.at[2], 2, 2, on_z(2 * side)).start()
 
+        def begin_near():
             @pl.loop(0, 2)
             def _(j):
                 one(1 + 6 * j)
@@ -268,6 +268,7 @@
             copy(final_kind, part.at[zz(1)], final.at[0], 0, 0, on_z(1)).start()
             copy(final_kind, part.at[zz(-1)], final.at[1], 1, 1, on_z(-1)).start()
 
+        def begin_own():
             @pl.loop(0, 3)
             def _(j):
                 one(j * (j + 1))
@@ -315,12 +316,13 @@
             for i in range(3):
                 left(far_kind, everything.at[z], i)
 
-        return begin, pass_on, publish, forward, collect, finish
+        return begin, pass_on, publish, forward, collect, finish, begin_near, begin_own
 
     back = over_z(B_RELAY, B_FINAL, B_NEAR, B_FAR, bpart, brelay, bfinal, ball, rga, ua, rgb, ub)
     low = over_z(L_RELAY, L_FINAL, L_NEAR, L_FAR, lpart, lrelay, lfinal, lall, rxa, da, rxb, db)
 
     route_x(0, 2, hold=True)
+    g_step(1)
     opposite_ring(FU_A, ua, x)
     opposite_ring(FU_B, ub, y)
 
@@ -331,8 +333,11 @@
         arrived(G_A, rga.at[fa], fa)
         arrived(G_B, rgb.at[fb], fb)
 
+    spread_ring(D_A, D_B, d_ref.at[:, pl.ds(0, HALF)], d_ref.at[:, pl.ds(HALF, HALF)], da, db)
     release_x(0, 2)
     back[0]()
+    back[6]()
+    back[7]()
     route_x(2, 4)
     back[1]()
     route_x(4, 6)
@@ -342,7 +347,6 @@
     forward_ring(D_A, FD_A, da, x, ring_x)
     forward_ring(D_B, FD_B, db, y, ring_y)
     back[4]()
-    g_step(1)
     opposite_ring(FD_A, da, x)
     opposite_ring(FD_B, db, y)
 
@@ -373,8 +377,7 @@
                 give_back(X_A, R_A, m_a, on_a, ma, True, da, sxa, reta, d)
                 give_back(X_B, R_B, m_b, on_b, mb, False, db, sxb, retb, d)
 
-    give_back_all(0, 8)
-    g_step(2)
+    give_back_all(0, 2)
 
     with jax.named_scope("wait_x"):
 
@@ -385,8 +388,13 @@
             arrived(X_A, rxa.at[fa], fa)
             arrived(X_B, rxb.at[fb], fb)
 
-    with jax.named_scope("low_parts"):
-        low[0]()
+    low[0]()
+    give_back_all(2, 4)
+    low[6]()
+    low[7]()
+    give_back_all(4, 6)
+    low[1]()
+    give_back_all(6, 8)
 
     def gradient(masked, rows, q):
         return adapter_scale * lax.dot_general(
@@ -431,28 +439,25 @@
             to_owners(DG_A, x, ring_x, ma, rxa, dga, dgra, dgo, 0, first)
             to_owners(DG_B, y, ring_y, mb, rxb, dgb, dgrb, dgo, 1, first)
 
-    low[1]()
     down_gradient(True)
-    g_step(3)
     low[2]()
 
-    with jax.named_scope("frozen"):
-        arrived(GR, g_half(-4, 0), 4)
-        arrived(GL, g_half(4, 1), 4)
-        w_in.wait()
-
-        @pl.loop(0, ROWS // TILE)
-        def _(i):
-            rows = pl.ds(pl.multiple_of(i * TILE, TILE), TILE)
-            acc[rows, :] = lax.dot_general(
-                gfull[rows, :], wv[...], (((1,), (1,)), ((), ())), preferred_element_type=F32
-            )
-
-    low[3]()
+    def frozen():
+        with jax.named_scope("frozen"):
+            arrived(GR, g_half(-4, 0), 4)
+            arrived(GL, g_half(4, 1), 4)
+            w_in.wait()
+
+            @pl.loop(0, ROWS // TILE)
+            def _(i):
+                rows = pl.ds(pl.multiple_of(i * TILE, TILE), TILE)
+                acc[rows, :] += lax.dot_general(
+                    gfull[rows, :], wv[...], (((1,), (1,)), ((), ())), preferred_element_type=F32
+                )
 
     lanes = lax.broadcasted_iota(jnp.int32, (TILE, SLOTS), 1)
 
-    def take(pair_number, last):
+    def take(pair_number, last=False):
         with jax.named_scope("take_back"):
             blocks = []
             for j in range(2):
@@ -473,7 +478,7 @@
                 slots = cols[rows, :].astype(jnp.int32)
                 for half, ret in enumerate((reta, retb)):
                     here = pl.ds(half * HALF, HALF)
-                    total = acc[rows, here]
+                    total = acc[rows, here] if pair_number else jnp.zeros((TILE, HALF), F32)
                     for ts in blocks:
                         t = ts[half]
                         pick = jnp.where(lanes + t * SLOTS == slots[:, half : half + 1], 1.0, 0.0).astype(BF)
@@ -498,11 +503,11 @@
             part[q] = value
             copy(kind, part.at[q], recv.at[m], q, m, ring(q)).start()
 
-    take(0, False)
-    take(1, False)
+    take(0)
+    low[3]()
+    g_step(2)
+    take(1)
     down_gradient(False)
-    take(2, False)
-    take(3, True)
     low[4]()
 
     with jax.named_scope("up_gradient"):
@@ -516,6 +521,11 @@
         def _(d):
             to_owner(UG_A, x, ring_x, ma, rga, uga, ugra, ugo, 0, d)
             to_owner(UG_B, y, ring_y, mb, rgb, ugb, ugrb, ugo, 1, d)
+
+    g_step(3)
+    take(2)
+    frozen()
+    take(3, True)
 
     with jax.named_scope("down_sum"):
         from_neighbours(DG_A, dgra, dgo, 0)

time: 132 us -> 121 us (0.917); the launches traced: 130 us -> 120 us
  Pallas kernels: 124 us -> 114 us
    pallas_call x1, Pallas kernels: 124 us -> 114 us  [adapter_backward(): pl.pallas_call(adapter_kernel, out_shape=(jax.ShapeDtypeStruct((ROWS, 2 *...]
where the time goes in v4:
time: 121 us; the launch traced here: 120 us
  Pallas kernels  114 us (94%)
  local copies, waits for them, and re-layouts  5.59 us (5%)
    pallas_call x1, Pallas kernels, adapter_backward(): pl.pallas_call(adapter_kernel, out_shape=(jax.ShapeDtypeStruct((ROWS, 2 *...  114 us
    unnamed x7, local copies, waits for them, and re-layouts  5.59 us

profile of v4, /device:TPU:6, one launch (start us, length us, event | category | flops | bytes accessed | tf_op | source)
XLA Modules:
  0.0 120.2 jit_solution(18358522064773742024)
XLA Ops:
  0.6 113.9 %adapter_backward.1 = (bf16[1536,1024]{1,0:T(8,128)(2,1)}, f32[256,1024]{1,0:T(8,128)}, f32[256,128]{1,0:T(8,128)}) custom-call(s32[1,1536]{1,0:T(1,128)} %bitcast.9, bf16[1536,1024]{1,0:T(8,128)(2,1)} %x_hbm.1, bf16[1536,128]{1,0:T(8,128)(2,1)} %g_ref.1, bf16[1024,1024]{1,0:T(8,128)(2,1)} %w_hbm.1, bf16[256,1024]{1,0:T(8,128)(2,1)} %bitcast.7, ...), custom_call_target="tpu_custom_call" | custom-call | flops 32000000000 | bytes 12000000 | tf_op jit(solution)/shard_map/adapter_backward/pallas_call | solution.py:606
  114.6 0.0 copy-start
  114.6 0.0 copy-start.1
  114.6 4.0 %copy.12 = bf16[1536,1024]{1,0:T(8,128)(2,1)} copy(bf16[1536,1024]{1,0:T(8,128)(2,1)} %get-tuple-element.12) | data formatting | bytes 6291456
  118.5 0.0 copy-done
  118.5 1.0 copy.13
  119.5 0.0 copy-done.1
  119.5 0.7 copy.14
Async XLA Ops:
  114.6 4.0 %copy-start = (f32[256,1024]{1,0:T(8,128)S(1)}, f32[256,1024]{1,0:T(8,128)}, u32[]{:S(2)}) copy-start(f32[256,1024]{1,0:T(8,128)} %get-tuple-element.7) | copy-start | bytes 3145732
  114.6 4.9 %copy-start.1 = (f32[256,128]{1,0:T(8,128)S(1)}, f32[256,128]{1,0:T(8,128)}, u32[]{:S(2)}) copy-start(f32[256,128]{1,0:T(8,128)} %get-tuple-element.8) | copy-start | bytes 393220

commit v5 on v4

--- a/solution.py
+++ b/solution.py
@@ -202,6 +202,7 @@
 
     gfull[:, g_cols(0)] = g_ref[...]
 
+    spread_ring(D_A, D_B, d_ref.at[:, pl.ds(0, HALF)], d_ref.at[:, pl.ds(HALF, HALF)], da, db)
     forward_ring(U_A, FU_A, ua, x, ring_x)
     forward_ring(U_B, FU_B, ub, y, ring_y)
     da[x] = d_ref[:, :HALF]
@@ -333,7 +334,6 @@
         arrived(G_A, rga.at[fa], fa)
         arrived(G_B, rgb.at[fb], fb)
 
-    spread_ring(D_A, D_B, d_ref.at[:, pl.ds(0, HALF)], d_ref.at[:, pl.ds(HALF, HALF)], da, db)
     release_x(0, 2)
     back[0]()
     back[6]()
@@ -392,14 +392,14 @@
     give_back_all(2, 4)
     low[6]()
     low[7]()
-    give_back_all(4, 6)
     low[1]()
-    give_back_all(6, 8)
+    give_back_all(4, 8)
 
     def gradient(masked, rows, q):
+        window = pl.ds(pl.multiple_of((q * 7) // 2 * 16, 16), 80)
         return adapter_scale * lax.dot_general(
-            masked[:, :, pl.ds(pl.multiple_of(q * OWN, OWN), OWN)].reshape(8 * SLOTS, OWN),
-            rows[...].reshape(8 * SLOTS, -1),
+            masked[:, window, pl.ds(pl.multiple_of(q * OWN, OWN), OWN)].reshape(8 * 80, OWN),
+            rows[:, window, :].reshape(8 * 80, -1),
             (((0,), (0,)), ((), ())),
             preferred_element_type=F32,
         )
@@ -439,8 +439,8 @@
             to_owners(DG_A, x, ring_x, ma, rxa, dga, dgra, dgo, 0, first)
             to_owners(DG_B, y, ring_y, mb, rxb, dgb, dgrb, dgo, 1, first)
 
+    low[2]()
     down_gradient(True)
-    low[2]()
 
     def frozen():
         with jax.named_scope("frozen"):
@@ -503,9 +503,9 @@
             part[q] = value
             copy(kind, part.at[q], recv.at[m], q, m, ring(q)).start()
 
-    take(0)
     low[3]()
     g_step(2)
+    take(0)
     take(1)
     down_gradient(False)
     low[4]()

time: 121 us -> 120 us (level)
  no operation moved by 1% of the time
where the time goes in v5:
time: 120 us
  Pallas kernels  114 us (95%)
  local copies, waits for them, and re-layouts  5.59 us (5%)
    pallas_call x1, Pallas kernels, adapter_backward(): pl.pallas_call(adapter_kernel, out_shape=(jax.ShapeDtypeStruct((ROWS, 2 *...  114 us
    unnamed x7, local copies, waits for them, and re-layouts  5.59 us

profile of v5, /device:TPU:6, one launch (start us, length us, event | category | flops | bytes accessed | tf_op | source)
XLA Modules:
  0.0 119.9 jit_solution(8102820362285747003)
XLA Ops:
  0.6 113.6 %adapter_backward.1 = (bf16[1536,1024]{1,0:T(8,128)(2,1)}, f32[256,1024]{1,0:T(8,128)}, f32[256,128]{1,0:T(8,128)}) custom-call(s32[1,1536]{1,0:T(1,128)} %bitcast.9, bf16[1536,1024]{1,0:T(8,128)(2,1)} %x_hbm.1, bf16[1536,128]{1,0:T(8,128)(2,1)} %g_ref.1, bf16[1024,1024]{1,0:T(8,128)(2,1)} %w_hbm.1, bf16[256,1024]{1,0:T(8,128)(2,1)} %bitcast.7, ...), custom_call_target="tpu_custom_call" | custom-call | flops 32000000000 | bytes 12000000 | tf_op jit(solution)/shard_map/adapter_backward/pallas_call | solution.py:606
  114.3 0.0 copy-start
  114.3 0.0 copy-start.1
  114.3 4.0 %copy.12 = bf16[1536,1024]{1,0:T(8,128)(2,1)} copy(bf16[1536,1024]{1,0:T(8,128)(2,1)} %get-tuple-element.12) | data formatting | bytes 6291456
  118.3 0.0 copy-done
  118.3 1.0 copy.13
  119.2 0.0 copy-done.1
  119.2 0.7 copy.14
Async XLA Ops:
  114.3 4.0 %copy-start = (f32[256,1024]{1,0:T(8,128)S(1)}, f32[256,1024]{1,0:T(8,128)}, u32[]{:S(2)}) copy-start(f32[256,1024]{1,0:T(8,128)} %get-tuple-element.7) | copy-start | bytes 3145732
  114.3 4.9 %copy-start.1 = (f32[256,128]{1,0:T(8,128)S(1)}, f32[256,128]{1,0:T(8,128)}, u32[]{:S(2)}) copy-start(f32[256,128]{1,0:T(8,128)} %get-tuple-element.8) | copy-start | bytes 393220
